TPU v7x, 128 devices: a whole 4x4x4 slice. The times are simulated.
128 devices in a mesh: strip: 128 (over z, x, y, core).
Axes of the slice: x: 4, y: 4, z: 4, core: 2. Of those that a mesh axis runs over, the one named last changes fastest.
Arguments:
- features: bfloat16 [128, 1920, 384], P(None, 'strip'), may hold values from -6 to 6
- grad_out: bfloat16 [128, 1920, 384], P(None, 'strip'), may hold values from -6 to 6
- widths: int32 [128], replicated, may hold values from 3 to 15, as said below
- dw_kernel: bfloat16 [49, 384], replicated, may hold values from -0.875 to 0.875
- dw_bias: bfloat16 [384], replicated, may hold values from -3 to 3
- ln_gain: bfloat16 [384], replicated, may hold values from 0.25 to 1.75
- ln_bias: bfloat16 [384], replicated, may hold values from -3 to 3
- w_in: bfloat16 [384, 1536], P(None, 'strip'), may hold values from -0.3125 to 0.3125
- in_bias: bfloat16 [1536], P('strip'), may hold values from -3 to 3
- w_out: bfloat16 [1536, 384], P('strip'), may hold values from -0.15625 to 0.15625
- out_bias: bfloat16 [384], replicated, may hold values from -3 to 3
- layer_scale: bfloat16 [384], replicated, may hold values from 0.5 to 2
Outputs:
- d_input: bfloat16 [128, 1920, 384], P(None, 'strip')
- g_dw_kernel: float32 [49, 384], replicated
- g_dw_bias: float32 [384], replicated
- g_ln_gain: float32 [384], replicated
- g_ln_bias: float32 [384], replicated
- g_w_in: float32 [384, 1536], P(None, 'strip')
- g_in_bias: float32 [1536], P('strip')
- g_w_out: float32 [1536, 384], P('strip')
- g_out_bias: float32 [384], replicated
- g_layer_scale: float32 [384], replicated
Inputs may be any that keep to these rules, and one draw needn't show every extreme that they name: Device d's strip fills its first widths[d] slots; strips lie side by side in device order and cover all 640 columns. Every aligned group of 8 devices (devices 8k to 8k+7) holds exactly 40 columns in all. Exactly one strip has 15 columns; every other strip is narrower.
All inputs are finite; a program needn't handle non-finite values.
Results may differ from a plain program's by a relative error of at most 0.009.
Values may be sent and summed in bfloat16 or wider, within the bound.
A program may use at most 128 MiB of HBM per device.

v0:
```python
import math

import jax
import jax.numpy as jnp
from jax import lax
from jax.sharding import PartitionSpec as P

COL_DEV = 5


inv_root_two = 0.7071067811865476
inv_root_tau = 0.3989422804014327
ln_eps = 1e-06


def shifted(block, axis, distance):
    devices = range(lax.axis_size(axis))
    route = [(i - distance, i) for i in devices if i - distance in devices]
    return lax.ppermute(block, axis, route)


def conv_taps(padded, kernel, row_count, col_count):
    summed = jnp.zeros((row_count, col_count, padded.shape[2]), jnp.float32)
    for tap_row in range(7):
        for tap_col in range(7):
            summed = (
                summed
                + kernel[tap_row * 7 + tap_col]
                * padded[tap_row : tap_row + row_count, tap_col : tap_col + col_count]
            )
    return summed


def kernel_terms(d_conv32, padded, row_count, col_count):
    return jnp.stack(
        [
            jnp.sum(
                d_conv32 * padded[tap_row : tap_row + row_count, tap_col : tap_col + col_count],
                axis=(0, 1),
            )
            for tap_row in range(7)
            for tap_col in range(7)
        ]
    )


def flipped(kernel):
    return kernel.reshape(7, 7, -1)[::-1, ::-1].reshape(49, -1)


def attach(strip_block, strip_width, from_left, from_right):
    row_count, slot_count, chan_count = strip_block.shape
    widened = jnp.concatenate(
        [from_left, strip_block, jnp.zeros((row_count, 3, chan_count), strip_block.dtype)], axis=1
    )
    widened = lax.dynamic_update_slice(
        widened, from_right, (jnp.int32(0), strip_width + 3, jnp.int32(0))
    )
    return jnp.pad(widened, ((3, 3), (0, 0), (0, 0)))


def mlp_back(conv_out, cotangent, w_in, in_bias, w_out, out_bias, ln_gain, ln_bias, layer_scale):
    values = conv_out.astype(jnp.float32)
    mean_val = jnp.mean(values, axis=-1, keepdims=True)
    centred = values - mean_val
    inv_std = lax.rsqrt(jnp.mean(centred * centred, axis=-1, keepdims=True) + ln_eps)
    normed_raw = centred * inv_std
    normed = (normed_raw * ln_gain.astype(jnp.float32) + ln_bias.astype(jnp.float32)).astype(
        jnp.bfloat16
    )
    pre_act = jnp.dot(normed, w_in, preferred_element_type=jnp.float32) + in_bias.astype(
        jnp.float32
    )
    cdf_part = 0.5 * (1.0 + lax.erf(pre_act * inv_root_two))
    activated = (pre_act * cdf_part).astype(jnp.bfloat16)
    mlp_out = jnp.dot(activated, w_out, preferred_element_type=jnp.float32) + out_bias.astype(
        jnp.float32
    )
    cot_wide = cotangent.astype(jnp.float32)
    g_scale = jnp.sum(cot_wide * mlp_out, axis=0)
    d_mlp = (cot_wide * layer_scale.astype(jnp.float32)).astype(jnp.bfloat16)
    g_obias = jnp.sum(d_mlp.astype(jnp.float32), axis=0)
    g_wout = lax.dot_general(
        activated, d_mlp, (((0,), (0,)), ((), ())), preferred_element_type=jnp.float32
    )
    d_act = lax.dot_general(
        d_mlp, w_out, (((1,), (1,)), ((), ())), preferred_element_type=jnp.float32
    )
    slope = cdf_part + pre_act * jnp.exp(-0.5 * pre_act * pre_act) * inv_root_tau
    d_pre = (d_act * slope).astype(jnp.bfloat16)
    g_ibias = jnp.sum(d_pre.astype(jnp.float32), axis=0)
    g_win = lax.dot_general(
        normed, d_pre, (((0,), (0,)), ((), ())), preferred_element_type=jnp.float32
    )
    d_norm = lax.dot_general(
        d_pre, w_in, (((1,), (1,)), ((), ())), preferred_element_type=jnp.float32
    )
    g_lgain = jnp.sum(d_norm * normed_raw, axis=0)
    g_lbias = jnp.sum(d_norm, axis=0)
    scaled = d_norm * ln_gain.astype(jnp.float32)
    d_conv = (
        inv_std
        * (
            scaled
            - jnp.mean(scaled, axis=-1, keepdims=True)
            - normed_raw * jnp.mean(scaled * normed_raw, axis=-1, keepdims=True)
        )
    ).astype(jnp.bfloat16)
    return (d_conv, (g_win, g_ibias, g_wout, g_obias, g_lgain, g_lbias, g_scale))


def local(
    features,
    grad_out,
    widths,
    dw_kernel,
    dw_bias,
    ln_gain,
    ln_bias,
    w_in,
    in_bias,
    w_out,
    out_bias,
    layer_scale,
):
    devices = lax.axis_size("strip")
    my_index = lax.axis_index("strip")
    row_count, slot_count, chan_count = features.shape
    strip_width = jnp.sum(jnp.where(jnp.arange(devices, dtype=jnp.int32) == my_index, widths, 0))
    w_in_full, in_bias_full, w_out_full = (
        lax.all_gather(w_in, "strip", axis=1, tiled=True),
        lax.all_gather(in_bias, "strip", axis=0, tiled=True),
        lax.all_gather(w_out, "strip", axis=0, tiled=True),
    )
    in_window = (jnp.arange(slot_count, dtype=jnp.int32) < strip_width)[None, :, None]
    feat_block = jnp.where(in_window, features, jnp.zeros_like(features))
    cot_block = jnp.where(in_window, grad_out, jnp.zeros_like(grad_out))
    feat_left = shifted(lax.dynamic_slice_in_dim(feat_block, strip_width - 3, 3, 1), "strip", 1)
    feat_right = shifted(feat_block[:, :3], "strip", -1)
    padded = attach(feat_block, strip_width, feat_left, feat_right).astype(jnp.float32)
    kernel = dw_kernel.astype(jnp.float32)
    conv_out = (
        conv_taps(padded, kernel, row_count, slot_count) + dw_bias.astype(jnp.float32)
    ).astype(jnp.bfloat16)
    d_flat, grads = mlp_back(
        conv_out.reshape(-1, chan_count),
        cot_block.reshape(-1, chan_count),
        w_in_full,
        in_bias_full,
        w_out_full,
        out_bias,
        ln_gain,
        ln_bias,
        layer_scale,
    )
    d_conv = d_flat.reshape(row_count, slot_count, chan_count)
    d_conv32 = d_conv.astype(jnp.float32)
    g_kernel = kernel_terms(d_conv32, padded, row_count, slot_count)
    g_dwbias = jnp.sum(d_conv32, axis=(0, 1))
    grad_left = shifted(lax.dynamic_slice_in_dim(d_conv, strip_width - 3, 3, 1), "strip", 1)
    grad_right = shifted(d_conv[:, :3], "strip", -1)
    d_padded = attach(d_conv, strip_width, grad_left, grad_right).astype(jnp.float32)
    d_local = cot_block.astype(jnp.float32) + conv_taps(
        d_padded, flipped(kernel), row_count, slot_count
    )
    d_input = jnp.where(in_window, d_local, 0.0).astype(jnp.bfloat16)
    g_win, g_ibias, g_wout, g_obias, g_lgain, g_lbias, g_scale = grads
    owned_win, owned_ibias, owned_wout = (
        lax.psum_scatter(g_win, "strip", scatter_dimension=1, tiled=True),
        lax.psum_scatter(g_ibias, "strip", scatter_dimension=0, tiled=True),
        lax.psum_scatter(g_wout, "strip", scatter_dimension=0, tiled=True),
    )
    sum_kernel, sum_dwbias, sum_lgain, sum_lbias, sum_obias, sum_scale = lax.psum(
        (g_kernel, g_dwbias, g_lgain, g_lbias, g_obias, g_scale), "strip"
    )
    grad_scale = 1.0 / math.sqrt(row_count * devices * COL_DEV)
    return (
        d_input,
        sum_kernel * grad_scale,
        sum_dwbias * grad_scale,
        sum_lgain * grad_scale,
        sum_lbias * grad_scale,
        owned_win * grad_scale,
        owned_ibias * grad_scale,
        owned_wout * grad_scale,
        sum_obias * grad_scale,
        sum_scale * grad_scale,
    )


def solution(mesh):
    placed = (
        P(None, "strip", None),
        P(None, "strip", None),
        P(),
        P(),
        P(),
        P(),
        P(),
        P(None, "strip"),
        P("strip"),
        P("strip", None),
        P(),
        P(),
    )
    return jax.shard_map(
        local,
        mesh=mesh,
        in_specs=placed,
        out_specs=(
            P(None, "strip", None),
            P(),
            P(),
            P(),
            P(),
            P(None, "strip"),
            P("strip"),
            P("strip", None),
            P(),
            P(),
        ),
        check_vma=False,
    )
```

profile of v0, /device:TPU:1, one launch (start us, length us, event | category | flops | bytes accessed | tf_op | source)
XLA Modules:
  0.0 1227.4 jit_solution(17141780614201662294)
XLA Ops:
  11.2 5.4 fusion.108
  17.9 4.6 collective-permute-start
  35.1 68.3 %all-reduce.2 = bf16[1536]{0:T(1024)(128)(2,1)S(1)} all-reduce(bf16[1536]{0:T(1024)(128)(2,1)S(1)} %dynamic-update-slice), channel_id=1, replica_groups=mesh['strip'=128] {'strip'}, use_global_device_ids=true, to_apply=%add.2 | all-reduce | flops 1536 | bytes 6144
  112.0 9.0 dynamic_update_slice.6
  126.0 114.7 %convert_reduce_fusion.3 = (f32[128,15]{1,0:T(8,128)S(1)}, bf16[128,15,384]{2,1,0:T(8,128)(2,1)S(1)}) fusion(f32[384]{0:T(512)} %convert_element_type.91, f32[134,21,384]{2,1,0:T(8,128)} %pad_convert_fusion.1, f32[384]{0:T(512)S(1)} %copy-done.69, f32[384]{0:T(512)S(1)} %copy-done.70, f32[384]{0:T(512)S(1)} %copy-done.71, f32[384]{0:T(512)S(1)} %copy-done.72, ...), kind=kLoop, calls=%fused_computation.228 | loop fusion | flops 74463360 | bytes 146065920 | tf_op jit(solution)/shard_map/reduce_sum | solution.py:64
  246.2 9.2 multiply_convert_fusion
  257.7 10.2 convert_reduce_fusion
  267.9 5.4 fusion.111
  274.4 5.0 fusion.109
  279.4 346.1 %fusion.113 = (f32[384,16]{0,1:T(8,128)S(1)}, f32[16,384]{1,0:T(8,128)S(1)}) fusion(f32[384,1536]{0,1:T(8,128)} %fusion.111, f32[1536,384]{1,0:T(8,128)} %fusion.109), kind=kCustom, calls=%all-reduce-scatter.2 | all-reduce-scatter fusion | flops 1572865 | bytes 4767744
  630.7 7.3 multiply_reduce_fusion.2
  647.9 33.6 %fusion.55 = (f32[384]{0:T(512)S(1)}, f32[384]{0:T(512)S(1)}, f32[384]{0:T(512)S(1)}, f32[384]{0:T(512)S(1)}, f32[384]{0:T(512)S(1)}, /*index=5*/f32[384]{0:T(51...) fusion(bf16[128,15,384]{2,1,0:T(8,128)(2,1)S(1)} %reshape.189, ...), kind=kLoop, calls=%fused_computation.106 | loop fusion | flops 27272448 | bytes 54586368 | tf_op jit(solution)/shard_map/reduce_sum | solution.py:37
  682.8 16.1 %collective-permute-start.44 = (f32[16,384]{1,0:T(8,128)S(1)}, f32[16,384]{1,0:T(8,128)S(1)}, u32[]{:S(2)}, u32[]{:S(2)}) collective-permute-start(f32[16,384]{1,0:T(8,128)S(1)} %get-tuple-element.190), channel_id=1, source_target_pairs={{0,9},{1,10},{2,11},{3,12},{4,13},{5,14},{6,15},{7,16},{8,17},{9,1... | collective-permute-start | bytes 73736
  700.2 9.0 collective-permute-start.46
  709.2 4.3 collective-permute-start.47
  713.5 33.9 %fusion.56 = (f32[384]{0:T(512)S(1)}, f32[384]{0:T(512)S(1)}, f32[384]{0:T(512)S(1)}, f32[384]{0:T(512)S(1)}, f32[384]{0:T(512)S(1)}, /*index=5*/f32[384]{0:T(51...) fusion(bf16[128,15,384]{2,1,0:T(8,128)(2,1)S(1)} %reshape.189, ...), kind=kLoop, calls=%fused_computation.107 | loop fusion | flops 27272448 | bytes 54586368 | tf_op jit(solution)/shard_map/reduce_sum | solution.py:37
  749.4 5.4 collective-permute-start.49
  758.7 4.5 collective-permute-start.51
  765.1 24.3 %fusion.54 = (f32[384]{0:T(512)S(1)}, f32[384]{0:T(512)S(1)}, f32[384]{0:T(512)S(1)}, f32[384]{0:T(512)S(1)}, f32[384]{0:T(512)S(1)}, /*index=5*/f32[384]{0:T(51...) fusion(bf16[128,15,384]{2,1,0:T(8,128)(2,1)S(1)} %reshape.189, ...), kind=kLoop, calls=%fused_computation.105 | loop fusion | flops 19901568 | bytes 39833088 | tf_op jit(solution)/shard_map/reduce_sum | solution.py:37
  800.0 6.0 multiply_reduce_fusion.1
  817.5 62.0 %all-reduce.8 = (f32[384]{0:T(512)S(1)}, f32[384]{0:T(512)S(1)}, f32[384]{0:T(512)S(1)}, f32[1536]{0:T(1024)S(1)}, f32[384]{0:T(512)S(1)}, /*index=5*/f32[384]{0:T(512)S(1)}) all-reduce(f32[384]{0:T(512)S(1)} %get-tuple-element.191, f32[384]{0:T(512)S(1)} %get-tuple-element.79, ...), channel_id=1, replica_groups=mesh['strip'=128] {'strip'}, use_global_device_ids=true, to_apply=%region_56.57 | all-reduce | flops 3456 | bytes 27648 | tf_op jit(solution)/shard_map/psum | solution.py:173
  879.5 5.2 collective-permute-start.63
  884.7 4.8 collective-permute-start.64
  909.4 4.6 collective-permute-start.15
  914.7 5.4 collective-permute-start.16
  951.3 4.4 stack.199
  966.4 7.3 concatenate.9
  992.9 21.3 %concatenate.8 = f32[384,524]{0,1:T(8,128)S(1)} concatenate(f32[384,12]{0,1:T(8,128)S(1)} %collective-permute-done.35, f32[384,16]{0,1:T(8,128)} %collective-permute-done.34, f32[384,16]{0,1:T(8,128)} %collective-permute-done.33, f32[384,16]{0,1:T(8,128)} %collective-permute-done.32, f32[384,16]{0,1:T(8,128)} %collective-permute-done.31, f32[384,16]{0,1:T(8,128)} %copy-done.28, ...), dimensions={1} | concatenate | bytes 1609728
  1014.8 73.0 %all-reduce.12.cloned.1.call-done = f32[49,384]{1,0:T(8,128)} async-done(((f32[49,384]{1,0:T(8,128)}), f32[49,384]{1,0:T(8,128)}) %all-reduce.12.cloned.1.call-update) | async-done | bytes 75280 | tf_op jit(solution)/shard_map/psum | solution.py:173
  1091.9 8.9 dynamic_update_slice.7
  1101.2 4.4 pad_convert_fusion
  1106.0 113.2 %fusion.60 = bf16[128,15,384]{2,1,0:T(8,128)(2,1)S(1)} fusion(f32[134,21,384]{2,1,0:T(8,128)} %pad_convert_fusion, f32[384]{0:T(512)S(1)} %copy-done.30, f32[384]{0:T(512)S(1)} %copy-done.31, f32[384]{0:T(512)S(1)} %copy-done.32, f32[384]{0:T(512)S(1)} %copy-done.33, f32[384]{0:T(512)S(1)} %copy-done.34, f32[384]{0:T(512)S(1)} %copy-done.35, ...), kind=kLoop, calls=%fused_computation.112 | loop fusion | flops 75202560 | bytes 147531280 | tf_op jit(solution)/shard_map/convert_element_type | solution.py:166
  (477 shorter events, 171.0 us)
Async XLA Ops:
  7.2 236.7 %all-gather.7.cloned.1.call-start = ((), (), s32[]{:S(2)}) async-start(), calls=%async_computation.2 | async-start | bytes 1585152 | tf_op jit(solution)/shard_map/all_gather | solution.py:131
  7.9 247.5 %all-gather.5.cloned.1.call-start = ((), (), s32[]{:S(2)}) async-start(), calls=%async_computation.1 | async-start | bytes 1585152 | tf_op jit(solution)/shard_map/all_gather | solution.py:133
  17.9 91.6 %collective-permute-start = (bf16[128,3,384]{2,1,0:T(4,128)(2,1)}, bf16[128,3,384]{2,1,0:T(4,128)(2,1)S(1)}, u32[]{:S(2)}, u32[]{:S(2)}) collective-permute-start(bf16[128,3,384]{2,1,0:T(4,128)(2,1)} %get-tuple-element.198), channel_id=1, source_target_pairs={{0,1},{1,2},{2,3},{3,4},{4,5},{5,6},{6,7},{7,8},{8,9},{9,10},{10,1... | collective-permute-start | bytes 884744 | tf_op jit(solution)/shard_map/ppermute | solution.py:19
  22.5 89.5 %collective-permute-start.1 = (bf16[128,3,384]{2,1,0:T(4,128)(2,1)}, bf16[128,3,384]{2,1,0:T(4,128)(2,1)}, u32[]{:S(2)}, u32[]{:S(2)}) collective-permute-start(bf16[128,3,384]{2,1,0:T(4,128)(2,1)} %get-tuple-element.197), channel_id=1, source_target_pairs={{1,0},{2,1},{3,2},{4,3},{5,4},{6,5},{7,6},{8,7},{9,8},{10,9},{11,1... | collective-permute-start | bytes 884744 | tf_op jit(solution)/shard_map/ppermute | solution.py:19
  24.5 1063.3 %all-reduce.12.cloned.1.call-start = ((), (), s32[]{:S(2)}) async-start(), calls=%async_computation | async-start | bytes 172032 | tf_op jit(solution)/shard_map/psum | solution.py:173
  625.5 19.7 %collective-permute-start.36 = (f32[16,384]{1,0:T(8,128)S(1)}, f32[16,384]{1,0:T(8,128)S(1)}, u32[]{:S(2)}, u32[]{:S(2)}) collective-permute-start(f32[16,384]{1,0:T(8,128)S(1)} %get-tuple-element.190), channel_id=1, source_target_pairs={{0,1},{1,2},{2,3},{3,4},{4,5},{5,6},{6,7},{7,8},{8,9},{9,10},{10,1... | collective-permute-start | bytes 73736
  629.0 52.5 %collective-permute-start.38 = (f32[16,384]{1,0:T(8,128)S(1)}, f32[16,384]{1,0:T(8,128)S(1)}, u32[]{:S(2)}, u32[]{:S(2)}) collective-permute-start(f32[16,384]{1,0:T(8,128)S(1)} %get-tuple-element.190), channel_id=1, source_target_pairs={{0,3},{1,4},{2,5},{3,6},{4,7},{5,8},{6,9},{7,10},{8,11},{9,12},{10... | collective-permute-start | bytes 73736
  642.6 40.1 %collective-permute-start.39 = (f32[16,384]{1,0:T(8,128)S(1)}, f32[16,384]{1,0:T(8,128)S(1)}, u32[]{:S(2)}, u32[]{:S(2)}) collective-permute-start(f32[16,384]{1,0:T(8,128)S(1)} %get-tuple-element.190), channel_id=1, source_target_pairs={{0,4},{1,5},{2,6},{3,7},{4,8},{5,9},{6,10},{7,11},{8,12},{9,13},{1... | collective-permute-start | bytes 73736
  644.0 54.9 %collective-permute-start.40 = (f32[16,384]{1,0:T(8,128)S(1)}, f32[16,384]{1,0:T(8,128)S(1)}, u32[]{:S(2)}, u32[]{:S(2)}) collective-permute-start(f32[16,384]{1,0:T(8,128)S(1)} %get-tuple-element.190), channel_id=1, source_target_pairs={{0,5},{1,6},{2,7},{3,8},{4,9},{5,10},{6,11},{7,12},{8,13},{9,14},{... | collective-permute-start | bytes 73736
  645.3 54.9 %collective-permute-start.41 = (f32[16,384]{1,0:T(8,128)S(1)}, f32[16,384]{1,0:T(8,128)S(1)}, u32[]{:S(2)}, u32[]{:S(2)}) collective-permute-start(f32[16,384]{1,0:T(8,128)S(1)} %get-tuple-element.190), channel_id=1, source_target_pairs={{0,6},{1,7},{2,8},{3,9},{4,10},{5,11},{6,12},{7,13},{8,14},{9,15},... | collective-permute-start | bytes 73736
  646.6 62.6 %collective-permute-start.42 = (f32[16,384]{1,0:T(8,128)S(1)}, f32[16,384]{1,0:T(8,128)S(1)}, u32[]{:S(2)}, u32[]{:S(2)}) collective-permute-start(f32[16,384]{1,0:T(8,128)S(1)} %get-tuple-element.190), channel_id=1, source_target_pairs={{0,7},{1,8},{2,9},{3,10},{4,11},{5,12},{6,13},{7,14},{8,15},{9,16}... | collective-permute-start | bytes 73736
  681.5 66.0 %collective-permute-start.43 = (f32[16,384]{1,0:T(8,128)S(1)}, f32[16,384]{1,0:T(8,128)S(1)}, u32[]{:S(2)}, u32[]{:S(2)}) collective-permute-start(f32[16,384]{1,0:T(8,128)S(1)} %get-tuple-element.190), channel_id=1, source_target_pairs={{0,8},{1,9},{2,10},{3,11},{4,12},{5,13},{6,14},{7,15},{8,16},{9,17... | collective-permute-start | bytes 73736
  682.8 66.6 %collective-permute-start.44 = (f32[16,384]{1,0:T(8,128)S(1)}, f32[16,384]{1,0:T(8,128)S(1)}, u32[]{:S(2)}, u32[]{:S(2)}) collective-permute-start(f32[16,384]{1,0:T(8,128)S(1)} %get-tuple-element.190), channel_id=1, source_target_pairs={{0,9},{1,10},{2,11},{3,12},{4,13},{5,14},{6,15},{7,16},{8,17},{9,1... | collective-permute-start | bytes 73736
  698.9 56.0 %collective-permute-start.45 = (f32[16,384]{1,0:T(8,128)S(1)}, f32[16,384]{1,0:T(8,128)S(1)}, u32[]{:S(2)}, u32[]{:S(2)}) collective-permute-start(f32[16,384]{1,0:T(8,128)S(1)} %get-tuple-element.190), channel_id=1, source_target_pairs={{0,10},{1,11},{2,12},{3,13},{4,14},{5,15},{6,16},{7,17},{8,18},{9,... | collective-permute-start | bytes 73736
  700.2 58.5 %collective-permute-start.46 = (f32[16,384]{1,0:T(8,128)S(1)}, f32[16,384]{1,0:T(8,128)S(1)}, u32[]{:S(2)}, u32[]{:S(2)}) collective-permute-start(f32[16,384]{1,0:T(8,128)S(1)} %get-tuple-element.190), channel_id=1, source_target_pairs={{0,11},{1,12},{2,13},{3,14},{4,15},{5,16},{6,17},{7,18},{8,19},{9,... | collective-permute-start | bytes 73736
  709.2 54.0 %collective-permute-start.47 = (f32[16,384]{1,0:T(8,128)S(1)}, f32[16,384]{1,0:T(8,128)S(1)}, u32[]{:S(2)}, u32[]{:S(2)}) collective-permute-start(f32[16,384]{1,0:T(8,128)S(1)} %get-tuple-element.190), channel_id=1, source_target_pairs={{0,12},{1,13},{2,14},{3,15},{4,16},{5,17},{6,18},{7,19},{8,20},{9,... | collective-permute-start | bytes 73736
  747.5 41.9 %collective-permute-start.48 = (f32[16,384]{1,0:T(8,128)S(1)}, f32[16,384]{1,0:T(8,128)S(1)}, u32[]{:S(2)}, u32[]{:S(2)}) collective-permute-start(f32[16,384]{1,0:T(8,128)S(1)} %get-tuple-element.190), channel_id=1, source_target_pairs={{0,13},{1,14},{2,15},{3,16},{4,17},{5,18},{6,19},{7,20},{8,21},{9,... | collective-permute-start | bytes 73736
  749.4 41.7 %collective-permute-start.49 = (f32[16,384]{1,0:T(8,128)S(1)}, f32[16,384]{1,0:T(8,128)S(1)}, u32[]{:S(2)}, u32[]{:S(2)}) collective-permute-start(f32[16,384]{1,0:T(8,128)S(1)} %get-tuple-element.190), channel_id=1, source_target_pairs={{0,14},{1,15},{2,16},{3,17},{4,18},{5,19},{6,20},{7,21},{8,22},{9,... | collective-permute-start | bytes 73736
  754.9 39.5 %collective-permute-start.50 = (f32[16,384]{1,0:T(8,128)S(1)}, f32[16,384]{1,0:T(8,128)S(1)}, u32[]{:S(2)}, u32[]{:S(2)}) collective-permute-start(f32[16,384]{1,0:T(8,128)S(1)} %get-tuple-element.190), channel_id=1, source_target_pairs={{0,15},{1,16},{2,17},{3,18},{4,19},{5,20},{6,21},{7,22},{8,23},{9,... | collective-permute-start | bytes 73736
  758.7 38.3 %collective-permute-start.51 = (f32[16,384]{1,0:T(8,128)S(1)}, f32[16,384]{1,0:T(8,128)S(1)}, u32[]{:S(2)}, u32[]{:S(2)}) collective-permute-start(f32[16,384]{1,0:T(8,128)S(1)} %get-tuple-element.190), channel_id=1, source_target_pairs={{0,16},{1,17},{2,18},{3,19},{4,20},{5,21},{6,22},{7,23},{8,24},{9,... | collective-permute-start | bytes 73736
  763.2 35.1 %collective-permute-start.52 = (f32[16,384]{1,0:T(8,128)S(1)}, f32[16,384]{1,0:T(8,128)S(1)}, u32[]{:S(2)}, u32[]{:S(2)}) collective-permute-start(f32[16,384]{1,0:T(8,128)S(1)} %get-tuple-element.190), channel_id=1, source_target_pairs={{0,17},{1,18},{2,19},{3,20},{4,21},{5,22},{6,23},{7,24},{8,25},{9,... | collective-permute-start | bytes 73736
  806.1 73.4 %collective-permute-start.58 = (f32[16,384]{1,0:T(8,128)S(1)}, f32[16,384]{1,0:T(8,128)S(1)}, u32[]{:S(2)}, u32[]{:S(2)}) collective-permute-start(f32[16,384]{1,0:T(8,128)S(1)} %get-tuple-element.190), channel_id=1, source_target_pairs={{0,23},{1,24},{2,25},{3,26},{4,27},{5,28},{6,29},{7,30},{8,31},{9,... | collective-permute-start | bytes 73736
  807.4 77.3 %collective-permute-start.59 = (f32[16,384]{1,0:T(8,128)S(1)}, f32[16,384]{1,0:T(8,128)S(1)}, u32[]{:S(2)}, u32[]{:S(2)}) collective-permute-start(f32[16,384]{1,0:T(8,128)S(1)} %get-tuple-element.190), channel_id=1, source_target_pairs={{0,24},{1,25},{2,26},{3,27},{4,28},{5,29},{6,30},{7,31},{8,32},{9,... | collective-permute-start | bytes 73736
  809.0 80.5 %collective-permute-start.60 = (f32[16,384]{1,0:T(8,128)S(1)}, f32[16,384]{1,0:T(8,128)S(1)}, u32[]{:S(2)}, u32[]{:S(2)}) collective-permute-start(f32[16,384]{1,0:T(8,128)S(1)} %get-tuple-element.190), channel_id=1, source_target_pairs={{0,25},{1,26},{2,27},{3,28},{4,29},{5,30},{6,31},{7,32},{8,33},{9,... | collective-permute-start | bytes 73736
  810.9 81.1 %collective-permute-start.61 = (f32[16,384]{1,0:T(8,128)S(1)}, f32[16,384]{1,0:T(8,128)S(1)}, u32[]{:S(2)}, u32[]{:S(2)}) collective-permute-start(f32[16,384]{1,0:T(8,128)S(1)} %get-tuple-element.190), channel_id=1, source_target_pairs={{0,26},{1,27},{2,28},{3,29},{4,30},{5,31},{6,32},{7,33},{8,34},{9,... | collective-permute-start | bytes 73736
  812.6 82.1 %collective-permute-start.62 = (f32[16,384]{1,0:T(8,128)S(1)}, f32[16,384]{1,0:T(8,128)}, u32[]{:S(2)}, u32[]{:S(2)}) collective-permute-start(f32[16,384]{1,0:T(8,128)S(1)} %get-tuple-element.190), channel_id=1, source_target_pairs={{0,27},{1,28},{2,29},{3,30},{4,31},{5,32},{6,33},{7,34},{8,35},{9,... | collective-permute-start | bytes 73736
  879.5 19.0 %collective-permute-start.63 = (f32[16,384]{1,0:T(8,128)S(1)}, f32[16,384]{1,0:T(8,128)}, u32[]{:S(2)}, u32[]{:S(2)}) collective-permute-start(f32[16,384]{1,0:T(8,128)S(1)} %get-tuple-element.190), channel_id=1, source_target_pairs={{0,28},{1,29},{2,30},{3,31},{4,32},{5,33},{6,34},{7,35},{8,36},{9,... | collective-permute-start | bytes 73736
  900.6 19.4 %collective-permute-start.12 = (f32[384,16]{0,1:T(8,128)S(1)}, f32[384,16]{0,1:T(8,128)S(1)}, u32[]{:S(2)}, u32[]{:S(2)}) collective-permute-start(f32[384,16]{0,1:T(8,128)S(1)} %get-tuple-element.189), channel_id=1, source_target_pairs={{0,9},{1,10},{2,11},{3,12},{4,13},{5,14},{6,15},{7,16},{8,17},{9,1... | collective-permute-start | bytes 73736
  961.7 20.9 %collective-permute-start.34 = (f32[384,16]{0,1:T(8,128)S(1)}, f32[384,16]{0,1:T(8,128)}, u32[]{:S(2)}, u32[]{:S(2)}) collective-permute-start(f32[384,16]{0,1:T(8,128)S(1)} %get-tuple-element.189), channel_id=1, source_target_pairs={{0,31},{1,32},{2,33},{3,34},{4,35},{5,36},{6,37},{7,38},{8,39},{9,... | collective-permute-start | bytes 73736
  963.6 22.6 %collective-permute-start.4 = (f32[384,16]{0,1:T(8,128)S(1)}, f32[384,16]{0,1:T(8,128)}, u32[]{:S(2)}, u32[]{:S(2)}) collective-permute-start(f32[384,16]{0,1:T(8,128)S(1)} %get-tuple-element.189), channel_id=1, source_target_pairs={{0,1},{1,2},{2,3},{3,4},{4,5},{5,6},{6,7},{7,8},{8,9},{9,10},{10,1... | collective-permute-start | bytes 73736
  988.3 101.1 %collective-permute-start.2 = (bf16[128,3,384]{2,1,0:T(4,128)(2,1)}, bf16[128,3,384]{2,1,0:T(4,128)(2,1)S(1)}, u32[]{:S(2)}, u32[]{:S(2)}) collective-permute-start(bf16[128,3,384]{2,1,0:T(4,128)(2,1)} %get-tuple-element.196), channel_id=1, source_target_pairs={{0,1},{1,2},{2,3},{3,4},{4,5},{5,6},{6,7},{7,8},{8,9},{9,10},{10,1... | collective-permute-start | bytes 884744 | tf_op jit(solution)/shard_map/ppermute | solution.py:19
  990.6 101.3 %collective-permute-start.3 = (bf16[128,3,384]{2,1,0:T(4,128)(2,1)S(1)}, bf16[128,3,384]{2,1,0:T(4,128)(2,1)}, u32[]{:S(2)}, u32[]{:S(2)}) collective-permute-start(bf16[128,3,384]{2,1,0:T(4,128)(2,1)S(1)} %get-tuple-element.195), channel_id=1, source_target_pairs={{1,0},{2,1},{3,2},{4,3},{5,4},{6,5},{7,6},{8,7},{9,8},{10,9},{11,1... | collective-permute-start | bytes 884744 | tf_op jit(solution)/shard_map/ppermute | solution.py:19
  (160 other events, 1970.6 us)
Sparse Core Ops, SparseCore 0:
  10.8 68.0 all-gather.6
  81.7 61.6 all-gather.4
  955.8 131.8 all-reduce.11
where the time goes:
time: 1240 us; the launch traced here: 1230 us
  blocking collectives  476 us (38%)
  other arithmetic  354 us (29%)
  starting transfers between devices  186 us (15%)
  local copies, waits for them, and re-layouts  74.9 us (6%)
  waiting for transfers between devices  73.9 us (6%)
  matrix products  43 us (3%)
  between operations  19.7 us (2%)
    unnamed x2, blocking collectives  414 us
    unnamed x64, starting transfers between devices  175 us
    reduce_sum x1, other arithmetic, mlp_back(): mean_val = jnp.mean(values, axis=-1, keepdims=True)  115 us
    convert_element_type x1, other arithmetic, local(): d_input = jnp.where(in_window, d_local, 0.0).astype(jnp.bfloat16)  113 us
    reduce_sum x3, other arithmetic, kernel_terms(): jnp.sum(d_conv32 * padded[tap_row:tap_row + row_count, tap_col:tap_col +...  91.8 us
    psum x1, waiting for transfers between devices, local(): lax.psum((g_kernel, g_dwbias, g_lgain, g_lbias, g_obias, g_scale), 'strip')  73 us
    psum x1, blocking collectives, local(): lax.psum((g_kernel, g_dwbias, g_lgain, g_lbias, g_obias, g_scale), 'strip')  62 us
    unnamed x251, local copies, waits for them, and re-layouts  37.1 us
  transfers between devices with their start and end apart: 71, of which 1 were waited for; matrix products, arithmetic and copies ran while one was open for 26% of the time, Pallas kernels for 0%

commit v1 on v0

v1 whole, which is shorter than its diff:
```python
import functools, math
import jax, jax.numpy as jnp
from jax import lax
from jax.sharding import PartitionSpec as P
from jax.experimental import pallas as pl
from jax.experimental.pallas import tpu as pltpu

ROWS, C, FF, CAP = 128, 384, 1536, 15
NCOL = 16
XCOL = NCOL + 6
RP = ROWS + 16
F32, BF16 = jnp.float32, jnp.bfloat16
VMEM = pl.BlockSpec(memory_space=pltpu.VMEM)
SMEM = pl.BlockSpec(memory_space=pltpu.SMEM)


def gelu_parts(x):
    e = jnp.exp(x * x * -0.5)
    t = 1.0 / (1.0 + (0.3275911 * 0.7071067811865476) * jnp.abs(x))
    q = ((((0.5 * 1.061405429) * t - 0.5 * 1.453152027) * t + 0.5 * 1.421413741) * t - 0.5 * 0.284496736) * t + 0.5 * 0.254829592
    h = q * t * e
    cdf = jnp.where(x >= 0, 1.0 - h, h)
    slope = cdf + x * e * 0.3989422804014327
    return x * cdf, slope


def fill_taps(taps_ref, tapb, flip):
    def body(i, _):
        src = 48 - i if flip else i
        row = taps_ref[pl.ds(src, 1), :]
        for g in range(3):
            tapb[i, g] = jnp.broadcast_to(row[:, g * 128:(g + 1) * 128], (8, 128))
        return 0
    lax.fori_loop(0, 49, body, 0)


def fill_ext(xf, own, from_left, from_right, n, has_left, has_right):
    zero = jnp.zeros((8, 128), F32)
    def edge(i, _):
        for g in range(3):
            xf[i, g, 0:8, :] = zero
            xf[i, g, RP - 8:RP, :] = zero
        return 0
    lax.fori_loop(0, XCOL, edge, 0)
    def put(dst, block):
        block = block.astype(F32)
        for g in range(3):
            xf[dst, g, 8:8 + ROWS, :] = block[:, g * 128:(g + 1) * 128]
    def blank(i, _):
        put(i, jnp.zeros((ROWS, C), BF16))
        return 0
    lax.fori_loop(n + 6, XCOL, blank, 0)
    def col(i, _):
        put(i + 3, own[i])
        return 0
    lax.fori_loop(0, n, col, 0)
    for i in range(3):
        put(i, jnp.where(has_left, from_left[i].astype(F32), 0.0))
        put(n + 3 + i, jnp.where(has_right, from_right[i].astype(F32), 0.0))


def conv_cols(xf, tapb, g, j0, r0, J):
    accs = [None] * J
    for a in range(7):
        xs = [xf[j0 + i, g, pl.ds(r0 + 5 + a, 8), :] for i in range(J + 6)]
        for b in range(7):
            t = tapb[a * 7 + b, g]
            for j in range(J):
                p = t * xs[j + b]
                accs[j] = p if accs[j] is None else accs[j] + p
    return accs


def k2_kernel(n_ref, feat, fl, fr, cot, taps, vecs, w1t_ref, w2t_ref,
              dconv, edge_l, edge_r, g1_out, g2_out, vec_out,
              xf, tapb, conv, w1, w2, g1, g2, vacc):
    n, has_left, has_right = n_ref[0], n_ref[1] > 0, n_ref[2] > 0
    fill_taps(taps, tapb, False)
    fill_ext(xf, feat, fl, fr, n, has_left, has_right)
    for f in range(FF // 256):
        sl = pl.ds(f * 256, 256)
        w1[:, sl] = w1t_ref[sl, :].T
        w2[:, sl] = w2t_ref[sl, :].T
    J = 4
    def jloop(jb, _):
        def gloop(g, _):
            bias = vecs[0:1, :]
            def rloop(r, _):
                r0 = r * 8
                accs = conv_cols(xf, tapb, g, jb * J, r0, J)
                for j in range(J):
                    conv[jb * J + j, g, pl.ds(pl.multiple_of(r0, 8), 8), :] = accs[j]
                return 0
            lax.fori_loop(0, 16, rloop, 0)
            return 0
        lax.fori_loop(0, 3, gloop, 0)
        return 0
    lax.fori_loop(0, (n + J - 1) // J, jloop, 0)

    bias, gain, lbias, ls = vecs[0:1, :], vecs[1:2, :], vecs[2:3, :], vecs[3:4, :]
    def zero_col(i, _):
        dconv[i] = jnp.zeros((ROWS, C), BF16)
        return 0
    lax.fori_loop(0, NCOL, zero_col, 0)
    vacc[...] = jnp.zeros_like(vacc)
    g1[...] = jnp.zeros_like(g1)
    g2[...] = jnp.zeros_like(g2)
    T = 2 * ROWS
    one_col = (lax.broadcasted_iota(jnp.int32, (T, 128), 1) == 0).astype(BF16)

    def part(x):
        return x.reshape(T // 8, 8, C).sum(0)

    def step(s, _):
        v = jnp.concatenate([conv[pl.ds(2 * s, 2), g].reshape(T, 128) for g in range(3)], axis=1) + bias
        v = v.astype(BF16).astype(F32)
        mean = jnp.sum(v, axis=1, keepdims=True) * (1.0 / C)
        cen = v - mean
        inv = lax.rsqrt(jnp.sum(cen * cen, axis=1, keepdims=True) * (1.0 / C) + 1e-6)
        nraw = cen * inv
        normed = jnp.concatenate([(nraw * gain + lbias).astype(BF16), one_col], axis=1)
        dm32 = cot[pl.ds(2 * s, 2)].reshape(T, C).astype(F32) * ls
        dmlp = dm32.astype(BF16)
        vacc[2] += part(dmlp.astype(F32))
        normed_t = normed.T
        dmlp_t = dmlp.T
        dn = jnp.zeros((T, C), F32)
        for f in range(FF // 256):
            sl = slice(f * 256, f * 256 + 256)
            pre = jnp.dot(normed, w1[:, sl], preferred_element_type=F32)
            dact = jnp.dot(dmlp, w2[:, sl], preferred_element_type=F32)
            act, slope = gelu_parts(pre)
            act = act.astype(BF16)
            dpre = (dact * slope).astype(BF16)
            g1[:, sl] += jnp.dot(normed_t, dpre, preferred_element_type=F32)
            g2[:, sl] += jnp.dot(dmlp_t, act, preferred_element_type=F32)
            dn += jnp.dot(dpre, w1t_ref[sl, 0:C], preferred_element_type=F32)
        vacc[0] += part(dn * nraw)
        vacc[1] += part(dn)
        sc = dn * gain
        m1 = jnp.sum(sc, axis=1, keepdims=True) * (1.0 / C)
        m2 = jnp.sum(sc * nraw, axis=1, keepdims=True) * (1.0 / C)
        dc = (inv * (sc - m1 - nraw * m2)).astype(BF16)
        vacc[4] += part(dc.astype(F32))
        dconv[pl.ds(2 * s, 2)] = dc.reshape(2, ROWS, C)
        return 0
    lax.fori_loop(0, (n + 1) // 2, step, 0)

    for i in range(3):
        edge_l[i] = dconv[i]
        edge_r[i] = dconv[n - 3 + i]
    srow = jnp.zeros((8, C), F32)
    for f in range(FF // 128):
        sl = slice(f * 128, f * 128 + 128)
        g1_out[sl, :] = g1[:, sl].T.astype(BF16)
        g2t = g2[:, sl].T
        g2_out[sl, :] = g2t.astype(BF16)
        srow += (g2t * w2t_ref[sl, :].astype(F32)).reshape(16, 8, C).sum(0)
    vacc[3] = srow
    rows = [jnp.sum(vacc[i], axis=0, keepdims=True) for i in range(5)]
    vec_out[...] = jnp.concatenate(rows + [jnp.zeros((3, C), F32)], axis=0)


def k2(n, feat, fl, fr, cot, taps, vecs, w1t, w2t):
    return pl.pallas_call(
        k2_kernel,
        out_shape=(
            jax.ShapeDtypeStruct((NCOL, ROWS, C), BF16),
            jax.ShapeDtypeStruct((3, ROWS, C), BF16),
            jax.ShapeDtypeStruct((3, ROWS, C), BF16),
            jax.ShapeDtypeStruct((FF, 512), BF16),
            jax.ShapeDtypeStruct((FF, C), BF16),
            jax.ShapeDtypeStruct((8, C), F32),
        ),
        in_specs=[SMEM] + [VMEM] * 8,
        out_specs=[VMEM] * 6,
        scratch_shapes=[
            pltpu.VMEM((XCOL, 3, RP, 128), F32),
            pltpu.VMEM((49, 3, 8, 128), F32),
            pltpu.VMEM((NCOL, 3, ROWS, 128), F32),
            pltpu.VMEM((512, FF), BF16),
            pltpu.VMEM((C, FF), BF16),
            pltpu.VMEM((512, FF), F32),
            pltpu.VMEM((C, FF), F32),
            pltpu.VMEM((8, 8, C), F32),
        ],
        compiler_params=pltpu.CompilerParams(vmem_limit_bytes=56 * 2**20),
        name="mlp_pass",
    )(n, feat, fl, fr, cot, taps, vecs, w1t, w2t)


def kernel_grads(xf, df, kacc, nb, J):
    def gloop(g, _):
        def aloop(a, _):
            def jloop(jb, accs):
                def rloop(r, accs):
                    r0 = r * 8
                    accs = list(accs)
                    ds = [df[jb * J + 3 + j, g, pl.ds(pl.multiple_of(r0 + 8, 8), 8), :] for j in range(J)]
                    xs = [xf[jb * J + i, g, pl.ds(r0 + 5 + a, 8), :] for i in range(J + 6)]
                    for b in range(7):
                        p = ds[0] * xs[b]
                        for j in range(1, J):
                            p = p + ds[j] * xs[j + b]
                        accs[b] = accs[b] + p
                    return tuple(accs)
                return lax.fori_loop(0, 16, rloop, accs, unroll=4)
            accs = lax.fori_loop(0, nb, jloop, tuple(jnp.zeros((8, 128), F32) for _ in range(7)))
            for b in range(7):
                kacc[a * 7 + b, g] = accs[b]
            return 0
        lax.fori_loop(0, 7, aloop, 0)
        return 0
    lax.fori_loop(0, 3, gloop, 0)


def k4_kernel(n_ref, feat, fl, fr, dconv, dl, dr, cot, taps, dimg, kg_out, xf, df, tapb, kacc):
    n, has_left, has_right = n_ref[0], n_ref[1] > 0, n_ref[2] > 0
    fill_taps(taps, tapb, True)
    fill_ext(xf, feat, fl, fr, n, has_left, has_right)
    zeros3 = jnp.zeros((3, ROWS, C), BF16)
    fill_ext(df, dconv, dl, zeros3, n, has_left, has_right)
    J = 4
    nb = (n + J - 1) // J
    kernel_grads(xf, df, kacc, nb, J)
    def kout(i, _):
        row = jnp.concatenate([jnp.sum(kacc[i, g], axis=0, keepdims=True) for g in range(3)], axis=1)
        kg_out[pl.ds(i, 1), :] = row
        return 0
    lax.fori_loop(0, 49, kout, 0)
    for i in range(3):
        block = jnp.where(has_right, dr[i].astype(F32), 0.0)
        for g in range(3):
            df[n + 3 + i, g, 8:8 + ROWS, :] = block[:, g * 128:(g + 1) * 128]

    def cjloop(jb, _):
        for g in range(3):
            ls = slice(g * 128, g * 128 + 128)
            def rloop(r, _):
                r0 = pl.multiple_of(r * 16, 16)
                lo = conv_cols(df, tapb, g, jb * J, r0, J)
                hi = conv_cols(df, tapb, g, jb * J, r0 + 8, J)
                for j in range(J):
                    col = jb * J + j
                    acc = jnp.concatenate([lo[j], hi[j]], axis=0) + cot[col, pl.ds(r0, 16), ls].astype(F32)
                    dimg[col, pl.ds(r0, 16), ls] = acc.astype(BF16)
                return 0
            lax.fori_loop(0, 8, rloop, 0)
        return 0
    lax.fori_loop(0, nb, cjloop, 0)
    def zero_col(i, _):
        dimg[i] = jnp.zeros((ROWS, C), BF16)
        return 0
    lax.fori_loop(n, NCOL, zero_col, 0)


def k4(n, feat, fl, fr, dconv, dl, dr, cot, taps):
    return pl.pallas_call(
        k4_kernel,
        out_shape=(
            jax.ShapeDtypeStruct((NCOL, ROWS, C), BF16),
            jax.ShapeDtypeStruct((56, C), F32),
        ),
        in_specs=[SMEM] + [VMEM] * 8,
        out_specs=[VMEM] * 2,
        scratch_shapes=[
            pltpu.VMEM((XCOL, 3, RP, 128), F32),
            pltpu.VMEM((XCOL, 3, RP, 128), F32),
            pltpu.VMEM((49, 3, 8, 128), F32),
            pltpu.VMEM((49, 3, 8, 128), F32),
        ],
        compiler_params=pltpu.CompilerParams(vmem_limit_bytes=56 * 2**20),
        name="conv_back",
    )(n, feat, fl, fr, dconv, dl, dr, cot, taps)


MESH = pl.DeviceIdType.MESH
N_DEV = 128


def place():
    me = lax.axis_index("strip")
    core = lax.rem(me, 2)
    y = lax.rem(me // 2, 4)
    x = lax.rem(me // 8, 4)
    z = me // 32
    return me, core, y, x, z


def peers_of(me, coord, stride):
    return [me + (lax.rem(coord + o, 4) - coord) * stride for o in (1, 2, 3)]


def greet(devices):
    barrier = pltpu.get_barrier_semaphore()
    for dev in devices:
        pl.semaphore_signal(barrier, inc=1, device_id=(dev,), device_id_type=MESH)
    pl.semaphore_wait(barrier, len(devices))


def send(src, dst, sems, idx, dev):
    copy = pltpu.make_async_remote_copy(
        src_ref=src, dst_ref=dst, send_sem=sems[0].at[idx], recv_sem=sems[1].at[idx],
        device_id=(dev,), device_id_type=MESH)
    copy.start()
    return copy


def wait_all(copies):
    for copy in copies:
        copy.wait()


def k1_kernel(s1, s2, el, er, w1_out, w2_out, fl_out, fr_out,
              bx1, bx2, w1, w2, fl, fr, ssem, rsem):
    me, core, y, x, z = place()
    xs, ys, zs = peers_of(me, x, 8), peers_of(me, y, 2), peers_of(me, z, 32)
    mate = me + 1 - 2 * core
    right, left = lax.rem(me + 1, N_DEV), lax.rem(me + N_DEV - 1, N_DEV)
    sems = (ssem, rsem)
    greet(xs + ys + zs + [mate, left, right])
    first = []
    for o in range(3):
        first.append(send(s1, bx1.at[x], sems, o, xs[o]))
        first.append(send(s2, bx2.at[x], sems, 3 + o, xs[o]))
    halo = [send(er, fl, sems, 6, right), send(el, fr, sems, 7, left)]
    bx1[x] = s1[...]
    bx2[x] = s2[...]
    wait_all(first)
    w1[core, z, y] = jnp.concatenate([bx1[q].astype(F32)[:12] for q in range(4)], axis=0).astype(BF16)
    w2[core, z, y] = jnp.concatenate([bx2[q].astype(F32)[:12] for q in range(4)], axis=0).astype(BF16)
    second = []
    for o in range(3):
        second.append(send(w1.at[core, z, y], w1.at[core, z, y], sems, 8 + o, ys[o]))
        second.append(send(w2.at[core, z, y], w2.at[core, z, y], sems, 11 + o, zs[o]))
    wait_all(second)
    third = []
    for o in range(3):
        third.append(send(w1.at[core, z], w1.at[core, z], sems, 14 + o, zs[o]))
        third.append(send(w2.at[core, :, y], w2.at[core, :, y], sems, 17 + o, ys[o]))
    wait_all(third)
    fourth = [send(w1.at[core], w1.at[core], sems, 20, mate), send(w2.at[core], w2.at[core], sems, 21, mate)]
    wait_all(halo)
    fl_out[...] = fl[...]
    fr_out[...] = fr[...]
    wait_all(fourth)
    w1_out[...] = w1[...]
    w2_out[...] = w2[...]


def k1(s1, s2, el, er):
    return pl.pallas_call(
        k1_kernel,
        out_shape=(
            jax.ShapeDtypeStruct((2, 4, 4, 48, 512), BF16),
            jax.ShapeDtypeStruct((2, 4, 4, 48, C), BF16),
            jax.ShapeDtypeStruct((3, ROWS, C), BF16),
            jax.ShapeDtypeStruct((3, ROWS, C), BF16),
        ),
        in_specs=[VMEM] * 4,
        out_specs=[VMEM] * 4,
        scratch_shapes=[
            pltpu.VMEM((4, 16, 512), BF16),
            pltpu.VMEM((4, 16, C), BF16),
            pltpu.VMEM((2, 4, 4, 48, 512), BF16),
            pltpu.VMEM((2, 4, 4, 48, C), BF16),
            pltpu.VMEM((3, ROWS, C), BF16),
            pltpu.VMEM((3, ROWS, C), BF16),
            pltpu.SemaphoreType.DMA((22,)),
            pltpu.SemaphoreType.DMA((22,)),
        ],
        compiler_params=pltpu.CompilerParams(collective_id=0, has_side_effects=True, vmem_limit_bytes=40 * 2**20),
        name="gather_weights",
    )(s1, s2, el, er)


def k3_kernel(g1, g2, el, er, o1, o2, fl_out, fr_out,
              rc1, rc2, c1, c2, rz1, ry2, t1, t2, ry1, rz2, p1, p2, rx1, rx2, fl, fr, ssem, rsem):
    me, core, y, x, z = place()
    xs, ys, zs = peers_of(me, x, 8), peers_of(me, y, 2), peers_of(me, z, 32)
    mate = me + 1 - 2 * core
    right, left = lax.rem(me + 1, N_DEV), lax.rem(me + N_DEV - 1, N_DEV)
    sems = (ssem, rsem)
    greet(xs + ys + zs + [mate, left, right])
    first = [send(g1.at[1 - core], rc1, sems, 0, mate), send(g2.at[1 - core], rc2, sems, 1, mate)]
    halo = [send(er, fl, sems, 2, right), send(el, fr, sems, 3, left)]
    wait_all(first)

    def add_first(i, _):
        zi, yi = i // 4, lax.rem(i, 4)
        c1[zi, yi] = (g1[core, zi, yi].astype(F32) + rc1[zi, yi].astype(F32)).astype(BF16)
        c2[zi, yi] = (g2[core, zi, yi].astype(F32) + rc2[zi, yi].astype(F32)).astype(BF16)
        return 0
    lax.fori_loop(0, 16, add_first, 0)
    second = []
    for o in range(3):
        second.append(send(c1.at[lax.rem(z + o + 1, 4)], rz1.at[o], sems, 4 + o, zs[o]))
        second.append(send(c2.at[:, lax.rem(y + o + 1, 4)], ry2.at[o], sems, 7 + o, ys[o]))
    wait_all(second)

    def add_second(i, _):
        t1[i] = (c1[z, i].astype(F32) + rz1[0, i].astype(F32) + rz1[1, i].astype(F32) + rz1[2, i].astype(F32)).astype(BF16)
        t2[i] = (c2[i, y].astype(F32) + ry2[0, i].astype(F32) + ry2[1, i].astype(F32) + ry2[2, i].astype(F32)).astype(BF16)
        return 0
    lax.fori_loop(0, 4, add_second, 0)
    third = []
    for o in range(3):
        third.append(send(t1.at[lax.rem(y + o + 1, 4)], ry1.at[o], sems, 10 + o, ys[o]))
        third.append(send(t2.at[lax.rem(z + o + 1, 4)], rz2.at[o], sems, 13 + o, zs[o]))
    wait_all(third)
    u1 = t1[y].astype(F32) + ry1[0].astype(F32) + ry1[1].astype(F32) + ry1[2].astype(F32)
    u2 = t2[z].astype(F32) + rz2[0].astype(F32) + rz2[1].astype(F32) + rz2[2].astype(F32)
    for q in range(4):
        p1[q, 0:12, :] = u1[q * 12:q * 12 + 12]
        p2[q, 0:12, :] = u2[q * 12:q * 12 + 12]
        p1[q, 12:16, :] = jnp.zeros((4, 512), F32)
        p2[q, 12:16, :] = jnp.zeros((4, C), F32)
    fourth = []
    for o in range(3):
        q = lax.rem(x + o + 1, 4)
        fourth.append(send(p1.at[q], rx1.at[o], sems, 16 + o, xs[o]))
        fourth.append(send(p2.at[q], rx2.at[o], sems, 19 + o, xs[o]))
    wait_all(halo)
    fl_out[...] = fl[...]
    fr_out[...] = fr[...]
    wait_all(fourth)
    o1[...] = p1[x] + rx1[0] + rx1[1] + rx1[2]
    o2[...] = p2[x] + rx2[0] + rx2[1] + rx2[2]


def k3(g1, g2, el, er):
    return pl.pallas_call(
        k3_kernel,
        out_shape=(
            jax.ShapeDtypeStruct((16, 512), F32),
            jax.ShapeDtypeStruct((16, C), F32),
            jax.ShapeDtypeStruct((3, ROWS, C), BF16),
            jax.ShapeDtypeStruct((3, ROWS, C), BF16),
        ),
        in_specs=[VMEM] * 4,
        out_specs=[VMEM] * 4,
        scratch_shapes=[
            pltpu.VMEM((4, 4, 48, 512), BF16),
            pltpu.VMEM((4, 4, 48, C), BF16),
            pltpu.VMEM((4, 4, 48, 512), BF16),
            pltpu.VMEM((4, 4, 48, C), BF16),
            pltpu.VMEM((3, 4, 48, 512), BF16),
            pltpu.VMEM((3, 4, 48, C), BF16),
            pltpu.VMEM((4, 48, 512), BF16),
            pltpu.VMEM((4, 48, C), BF16),
            pltpu.VMEM((3, 48, 512), BF16),
            pltpu.VMEM((3, 48, C), BF16),
            pltpu.VMEM((4, 16, 512), F32),
            pltpu.VMEM((4, 16, C), F32),
            pltpu.VMEM((3, 16, 512), F32),
            pltpu.VMEM((3, 16, C), F32),
            pltpu.VMEM((3, ROWS, C), BF16),
            pltpu.VMEM((3, ROWS, C), BF16),
            pltpu.SemaphoreType.DMA((22,)),
            pltpu.SemaphoreType.DMA((22,)),
        ],
        compiler_params=pltpu.CompilerParams(collective_id=1, has_side_effects=True, vmem_limit_bytes=40 * 2**20),
        name="scatter_grads",
    )(g1, g2, el, er)


def k5_kernel(kg, vec, out, cur, slots, ssem, rsem):
    me, core, y, x, z = place()
    xs, ys, zs = peers_of(me, x, 8), peers_of(me, y, 2), peers_of(me, z, 32)
    mate = me + 1 - 2 * core
    sems = (ssem, rsem)
    greet(xs + ys + zs + [mate])
    cur[0, 0:56, :] = kg[...]
    cur[0, 56:64, :] = vec[...]
    at = 0
    for stage, group in enumerate(([mate], ys, zs, xs)):
        copies = []
        for dev in group:
            copies.append(send(cur.at[stage], slots.at[at], sems, at, dev))
            at += 1
        wait_all(copies)
        total = cur[stage]
        for i in range(len(group)):
            total = total + slots[at - len(group) + i]
        if stage == 3:
            out[...] = total
        else:
            cur[stage + 1] = total


def k5(kg, vec):
    return pl.pallas_call(
        k5_kernel,
        out_shape=jax.ShapeDtypeStruct((64, C), F32),
        in_specs=[VMEM] * 2,
        out_specs=VMEM,
        scratch_shapes=[
            pltpu.VMEM((4, 64, C), F32),
            pltpu.VMEM((10, 64, C), F32),
            pltpu.SemaphoreType.DMA((10,)),
            pltpu.SemaphoreType.DMA((10,)),
        ],
        compiler_params=pltpu.CompilerParams(collective_id=2, has_side_effects=True),
        name="sum_vectors",
    )(kg, vec)


def local(features, grad_out, widths, dw_kernel, dw_bias, ln_gain, ln_bias,
          w_in, in_bias, w_out, out_bias, layer_scale):
    me = lax.axis_index("strip")
    n = lax.dynamic_index_in_dim(widths, me, keepdims=False)
    scal = jnp.stack([n, (me > 0).astype(jnp.int32), (me < N_DEV - 1).astype(jnp.int32)])
    mask = (jnp.arange(CAP, dtype=jnp.int32) < n)[:, None, None]

    def columns(a):
        a = jnp.where(mask, jnp.transpose(a, (1, 0, 2)), jnp.zeros((), a.dtype))
        return jnp.pad(a, ((0, NCOL - CAP), (0, 0), (0, 0)))
    feat, cot = columns(features), columns(grad_out)
    el = feat[:3]
    er = lax.dynamic_slice_in_dim(feat, n - 3, 3, 0)
    s1 = jnp.pad(jnp.concatenate([w_in.T, in_bias[:, None]], axis=1), ((0, 4), (0, 127)))
    s2 = jnp.pad(w_out, ((0, 4), (0, 0)))
    taps = dw_kernel.astype(F32)
    vecs = jnp.pad(jnp.stack([dw_bias, ln_gain, ln_bias, layer_scale]).astype(F32), ((0, 4), (0, 0)))
    w1t, w2t, fl, fr = k1(s1, s2, el, er)
    dconv, del_, der, g1, g2, vec = k2(scal, feat, fl, fr, cot, taps, vecs,
                                       w1t.reshape(FF, 512), w2t.reshape(FF, C))
    o1, o2, dl, dr = k3(g1.reshape(2, 4, 4, 48, 512), g2.reshape(2, 4, 4, 48, C), del_, der)
    dimg, kg = k4(scal, feat, fl, fr, dconv, dl, dr, cot, taps)
    total = k5(kg, vec)
    s = 1.0 / math.sqrt(ROWS * N_DEV * 5)
    ls, ob = layer_scale.astype(F32), out_bias.astype(F32)
    g_scale = (total[59] + ob * total[58]) / ls
    d_input = jnp.transpose(dimg[:CAP], (1, 0, 2))
    return (d_input, total[:49] * s, total[60] * s, total[56] * s, total[57] * s,
            o1[:12, :C].T * s, o1[:12, C] * s, o2[:12] * s, total[58] * s, g_scale * s)


def solution(mesh):
    wide = P(None, "strip", None)
    return jax.shard_map(
        local, mesh=mesh,
        in_specs=(wide, wide, P(), P(), P(), P(), P(), P(None, "strip"), P("strip"), P("strip", None), P(), P()),
        out_specs=(wide, P(), P(), P(), P(), P(None, "strip"), P("strip"), P("strip", None), P(), P()),
        check_vma=False)
```

time: 1240 us -> 205 us (0.17)
  blocking collectives: 476 us -> 0 us
  other arithmetic: 354 us -> 11.7 us
  starting transfers between devices: 186 us -> 0 us
  Pallas kernels: 0 us -> 168 us
  waiting for transfers between devices: 73.9 us -> 0 us
  local copies, waits for them, and re-layouts: 74.9 us -> 20.6 us
  matrix products: 43 us -> 0 us
  between operations: 19.7 us -> 2.03 us
    unnamed x2 -> x0, blocking collectives: 414 us -> none
    reduce_sum x8 -> x0, other arithmetic: 211 us -> none  [the longest x1 115 us: mlp_back(): mean_val = jnp.mean(values, axis=-1, keepdims=True)]
    unnamed x64 -> x0, starting transfers between devices: 175 us -> none
    pallas_call x0 -> x5, Pallas kernels: none -> 168 us  [the longest x1 59 us: k3(): pl.pallas_call(k3_kernel, out_shape=(jax.ShapeDtypeStruct((16, 512), F32)...]
    convert_element_type x11 -> x1, other arithmetic: 130 us -> 1.43 us  [local(): taps = dw_kernel.astype(F32)]
    psum x1 -> x0, waiting for transfers between devices: 73 us -> none  [local(): lax.psum((g_kernel, g_dwbias, g_lgain, g_lbias, g_obias, g_scale), 'strip')]
    psum x1 -> x0, blocking collectives: 62 us -> none  [local(): lax.psum((g_kernel, g_dwbias, g_lgain, g_lbias, g_obias, g_scale), 'strip')]
    dot_general x6 -> x0, matrix products: 43 us -> none  [the longest x1 10.2 us: mlp_back(): lax.dot_general(d_mlp, w_out, (((1,), (1,)), ((), ())), preferred_element...]
  transfers between devices with their start and end apart: 71 -> 0, of which waited for: 1 -> 0; matrix products, arithmetic and copies ran while one was open for 26% -> 0% of each run, Pallas kernels for 0% -> 0%
where the time goes in v1:
time: 205 us; the launch traced here: 203 us
  Pallas kernels  168 us (82%)
  local copies, waits for them, and re-layouts  20.6 us (10%)
  other arithmetic  11.7 us (6%)
    pallas_call x1, Pallas kernels, k3(): pl.pallas_call(k3_kernel, out_shape=(jax.ShapeDtypeStruct((16, 512), F32)...  59 us
    pallas_call x1, Pallas kernels, k5(): pl.pallas_call(k5_kernel, out_shape=jax.ShapeDtypeStruct((64, C), F32), i...  43.4 us
    pallas_call x1, Pallas kernels, k1(): pl.pallas_call(k1_kernel, out_shape=(jax.ShapeDtypeStruct((2, 4, 4, 48, 5...  31.4 us
    pallas_call x1, Pallas kernels, k2(): pl.pallas_call(k2_kernel, out_shape=(jax.ShapeDtypeStruct((NCOL, ROWS, C)...  20.7 us
    pallas_call x1, Pallas kernels, k4(): pl.pallas_call(k4_kernel, out_shape=(jax.ShapeDtypeStruct((NCOL, ROWS, C)...  13.8 us
    unnamed x24, local copies, waits for them, and re-layouts  9.66 us

profile of v1, /device:TPU:1, one launch (start us, length us, event | category | flops | bytes accessed | tf_op | source)
XLA Modules:
  0.0 202.6 jit_solution(1186805176123778067)
XLA Ops:
  0.6 1.2 dynamic_slice.7
  3.2 1.2 pad_add_fusion.n_ref
  4.4 0.6 iota_compare_fusion.3
  5.1 0.7 stack.36
  5.8 0.7 stack.37
  6.4 0.7 stack.38
  7.1 0.7 stack.39
  7.8 0.7 copy.23
  9.2 0.7 fusion.5.s1
  9.9 0.7 pad.23.s2
  10.6 1.4 convert_element_type.21.taps
  12.0 2.2 %select_bitcast_fusion = (bf16[15,128,384]{2,1,0:T(8,128)(2,1)S(1)}, bf16[15,128,384]{2,1,0:T(8,128)(2,1)S(1)}) fusion(bf16[128,15,384]{2,0,1:T(8,128)(2,1)} %param.13, pred[15]{0:T(512)(128)(4,1)S(1)} %iota_compare_fusion.3, bf16[128,15,384]{2,0,1:T(8,128)(2,1)} %param.12), kind=kLoop, calls=%fused_computation.1 | loop fusion | flops 1474560 | bytes 5898255 | tf_op jit(solution)/shard_map/jit(_where)/select_n | solution.py:516
  14.2 1.4 pad.24.cot
  15.6 1.4 pad.21.feat
  17.0 31.4 %gather_weights.1 = (bf16[2,4,4,48,512]{4,3,2,1,0:T(8,128)(2,1)S(1)}, bf16[2,4,4,48,384]{4,3,2,1,0:T(8,128)(2,1)S(1)}, bf16[3,128,384]{2,1,0:T(8,128)(2,1)S(1)}, bf16[3,128,384]{2,1,0:T(8,128)(2,1)S(1)}) custom-call(bf16[16,512]{1,0:T(8,128)(2,1)S(1)} %fusion.5.s1, bf16[16,384]{1,0:T(8,128)(2,1)S(1)} %pad.23.s2, ...), custom_call_target="tpu_custom_call" | custom-call | tf_op jit(solution)/shard_map/gather_weights/pallas_call | solution.py:352
  48.4 1.1 copy-done.1
  49.5 1.0 copy-done.3
  50.6 0.7 copy-done.4
  51.3 0.7 copy-done.5
  52.0 20.7 %mlp_pass.1 = (bf16[16,128,384]{2,1,0:T(8,128)(2,1)}, bf16[3,128,384]{2,1,0:T(8,128)(2,1)}, bf16[3,128,384]{2,1,0:T(8,128)(2,1)}, bf16[1536,512]{1,0:T(8,128)(2,...) custom-call(s32[3]{0:T(128)} %pad_add_fusion.n_ref, bf16[16,128,384]{2,1,0:T(8,128)(2,1)} %pad.21.feat, ...), custom_call_target="tpu_custom_call" | custom-call | tf_op jit(solution)/shard_map/mlp_pass/pallas_call | solution.py:165
  72.7 1.4 copy-done
  74.1 1.3 copy-done.2
  75.4 1.0 copy-done.6
  76.4 1.0 copy-done.7
  77.3 59.0 %scatter_grads.1 = (f32[16,512]{1,0:T(8,128)S(1)}, f32[16,384]{1,0:T(8,128)S(1)}, bf16[3,128,384]{2,1,0:T(8,128)(2,1)S(1)}, bf16[3,128,384]{2,1,0:T(8,128)(2,1)S(1)}) custom-call(bf16[2,4,4,48,512]{4,3,2,1,0:T(8,128)(2,1)S(1)} %bitcast.17, bf16[2,4,4,48,384]{4,3,2,1,0:T(8,128)(2,1)S(1)} %bitcast.19, bf16[3,128,384]{2,1,0:T(8,128)(2,1)S(1)} %copy-done.6, ...), custom_call_target="tpu_custom_call" | custom-call | tf_op jit(solution)/shard_map/scatter_grads/pallas_call | solution.py:432
  136.4 0.7 copy-done.8
  137.1 0.7 copy-done.9
  137.8 13.8 %conv_back.1 = (bf16[16,128,384]{2,1,0:T(8,128)(2,1)}, f32[56,384]{1,0:T(8,128)}) custom-call(s32[3]{0:T(128)} %pad_add_fusion.n_ref, bf16[16,128,384]{2,1,0:T(8,128)(2,1)} %pad.21.feat, bf16[3,128,384]{2,1,0:T(8,128)(2,1)} %copy-done.4, bf16[3,128,384]{2,1,0:T(8,128)(2,1)} %copy-done.5, bf16[16,128,384]{2,1,0:T(8,128)(2,1)} %get-tuple-element.30.dconv, ...), custom_call_target="tpu_custom_call" | custom-call | tf_op jit(solution)/shard_map/conv_back/pallas_call | solution.py:258
  151.6 2.7 %slice_bitcast_fusion = bf16[128,15,384]{2,0,1:T(8,128)(2,1)} fusion(bf16[16,128,384]{2,1,0:T(8,128)(2,1)} %get-tuple-element.37), kind=kLoop, calls=%fused_computation | loop fusion | bytes 2949120 | tf_op jit(solution)/shard_map/transpose | solution.py:534
  155.6 43.4 %sum_vectors.1 = f32[64,384]{1,0:T(8,128)} custom-call(f32[56,384]{1,0:T(8,128)} %get-tuple-element.38.kg, f32[8,384]{1,0:T(8,128)} %get-tuple-element.39.vec), custom_call_target="tpu_custom_call" | custom-call | tf_op jit(solution)/shard_map/sum_vectors/pallas_call | solution.py:492
  199.0 1.5 slice_reduce_fusion
  200.5 1.5 slice_multiply_fusion
  (19 shorter events, 2.6 us)
Async XLA Ops:
  48.4 1.2 copy-start.1
  49.5 1.0 copy-start.3
  50.6 0.7 copy-start.4
  51.3 0.7 copy-start.5
  72.7 1.4 copy-start
  74.1 1.3 copy-start.2
  75.4 1.0 copy-start.6
  76.4 1.0 copy-start.7
  136.4 0.7 copy-start.8
  137.1 0.7 copy-start.9
  151.6 50.4 %copy-start.10 = (bf16[384]{0:T(512)(128)(2,1)S(1)}, bf16[384]{0:T(512)(128)(2,1)}, u32[]{:S(2)}) copy-start(bf16[384]{0:T(512)(128)(2,1)} %param.23) | copy-start | bytes 2308
  151.6 50.4 %copy-start.11 = (bf16[384]{0:T(512)(128)(2,1)S(1)}, bf16[384]{0:T(512)(128)(2,1)}, u32[]{:S(2)}) copy-start(bf16[384]{0:T(512)(128)(2,1)} %param.22) | copy-start | bytes 2308

commit v2 on v0

v2 whole, which is shorter than its diff:
```python
import math

import jax
import jax.numpy as jnp
from jax import lax
from jax.sharding import PartitionSpec as P
from jax.experimental import pallas as pl
from jax.experimental.pallas import tpu as pltpu

ROWS, C, FF, CAP = 128, 384, 1536, 15
N_DEV = 128
NC = 12
XC = NC + 6
RP = ROWS + 16
J = 4
T = 2 * ROWS
F32, BF16 = jnp.float32, jnp.bfloat16
VMEM = pl.BlockSpec(memory_space=pltpu.VMEM)
SMEM = pl.BlockSpec(memory_space=pltpu.SMEM)
MESH = pl.DeviceIdType.MESH
SCALE = 1.0 / math.sqrt(ROWS * N_DEV * 5)


def gelu_parts(x):
    e = jnp.exp(x * x * -0.5)
    t = 1.0 / (1.0 + (0.3275911 * 0.7071067811865476) * jnp.abs(x))
    q = ((((0.5 * 1.061405429) * t - 0.5 * 1.453152027) * t + 0.5 * 1.421413741) * t - 0.5 * 0.284496736) * t + 0.5 * 0.254829592
    h = q * t * e
    cdf = jnp.where(x >= 0, 1.0 - h, h)
    slope = cdf + x * e * 0.3989422804014327
    return x * cdf, slope


def fill_taps(taps_ref, tapb, flip):
    for g in range(3):
        block = taps_ref[:, g * 128:(g + 1) * 128].astype(F32)
        for i in range(49):
            src = 48 - i if flip else i
            tapb[i, g] = jnp.broadcast_to(block[src:src + 1], (8, 128))


def put_column(xf, dst, block):
    block = block.astype(F32)
    for g in range(3):
        xf[dst, g, 8:8 + ROWS, :] = block[:, g * 128:(g + 1) * 128]


def clear_pads(xf):
    zero = jnp.zeros((8, 128), F32)

    def body(i, _):
        for g in range(3):
            xf[i, g, 0:8, :] = zero
            xf[i, g, RP - 8:RP, :] = zero
        return 0
    lax.fori_loop(0, XC, body, 0)


def conv_cols(xf, tapb, g, j0, r0):
    accs = [None] * J
    for a in range(7):
        xs = [xf[j0 + i, g, pl.ds(r0 + 5 + a, 8), :] for i in range(J + 6)]
        for b in range(7):
            t = tapb[a * 7 + b, g]
            for j in range(J):
                p = t * xs[j + b]
                accs[j] = p if accs[j] is None else accs[j] + p
    return accs


def conv_block(xf, tapb, conv, jb):
    def gloop(g, _):
        def rloop(r, _):
            r0 = r * 8
            accs = conv_cols(xf, tapb, g, jb * J, r0)
            for j in range(J):
                conv[jb * J + j, g, pl.ds(pl.multiple_of(r0, 8), 8), :] = accs[j]
            return 0
        lax.fori_loop(0, 16, rloop, 0)
        return 0
    lax.fori_loop(0, 3, gloop, 0)


def back_block(df, tapb, cotb, dimg, jb):
    for g in range(3):
        ls = slice(g * 128, g * 128 + 128)

        def rloop(r, _):
            r0 = pl.multiple_of(r * 16, 16)
            lo = conv_cols(df, tapb, g, jb * J, r0)
            hi = conv_cols(df, tapb, g, jb * J, r0 + 8)
            for j in range(J):
                col = jb * J + j
                acc = jnp.concatenate([lo[j], hi[j]], axis=0) + cotb[col, pl.ds(r0, 16), ls].astype(F32)
                dimg[col, pl.ds(r0, 16), ls] = acc.astype(BF16)
            return 0
        lax.fori_loop(0, 8, rloop, 0)


def kernel_grads(xf, df, kacc, g):
    def aloop(a, _):
        def jloop(jb, accs):
            def rloop(r, accs):
                r0 = r * 8
                accs = list(accs)
                ds = [df[jb * J + 3 + j, g, pl.ds(pl.multiple_of(r0 + 8, 8), 8), :] for j in range(J)]
                xs = [xf[jb * J + i, g, pl.ds(r0 + 5 + a, 8), :] for i in range(J + 6)]
                for b in range(7):
                    p = ds[0] * xs[b]
                    for j in range(1, J):
                        p = p + ds[j] * xs[j + b]
                    accs[b] = accs[b] + p
                return tuple(accs)
            return lax.fori_loop(0, 16, rloop, accs, unroll=4)
        accs = lax.fori_loop(0, NC // J, jloop, tuple(jnp.zeros((8, 128), F32) for _ in range(7)))
        for b in range(7):
            kacc[a * 7 + b, g] = accs[b]
        return 0
    lax.fori_loop(0, 7, aloop, 0)


def part(x):
    return x.reshape(T // 8, 8, C).sum(0)


def mlp_step(s, conv, cotb, vecs, w1, w2, w1t, g1, g2, vacc, dcv):
    bias, gain, lbias, ls = vecs
    one_col = (lax.broadcasted_iota(jnp.int32, (T, 128), 1) == 0).astype(BF16)
    v = jnp.concatenate([conv[pl.ds(2 * s, 2), g].reshape(T, 128) for g in range(3)], axis=1) + bias
    v = v.astype(BF16).astype(F32)
    mean = jnp.sum(v, axis=1, keepdims=True) * (1.0 / C)
    cen = v - mean
    inv = lax.rsqrt(jnp.sum(cen * cen, axis=1, keepdims=True) * (1.0 / C) + 1e-6)
    nraw = cen * inv
    normed = jnp.concatenate([(nraw * gain + lbias).astype(BF16), one_col], axis=1)
    dmlp = (cotb[pl.ds(2 * s, 2)].reshape(T, C).astype(F32) * ls).astype(BF16)
    vacc[2] += part(dmlp.astype(F32))
    normed_t = normed.T
    dmlp_t = dmlp.T
    dn = jnp.zeros((T, C), F32)
    for f in range(FF // 256):
        sl = slice(f * 256, f * 256 + 256)
        pre = jnp.dot(normed, w1[:, sl], preferred_element_type=F32)
        dact = jnp.dot(dmlp, w2[:, sl], preferred_element_type=F32)
        act, slope = gelu_parts(pre)
        act = act.astype(BF16)
        dpre = (dact * slope).astype(BF16)
        g1[:, sl] += jnp.dot(normed_t, dpre, preferred_element_type=F32)
        g2[:, sl] += jnp.dot(dmlp_t, act, preferred_element_type=F32)
        dn += jnp.dot(dpre, w1t[f], preferred_element_type=F32)
    vacc[0] += part(dn * nraw)
    vacc[1] += part(dn)
    sc = dn * gain
    m1 = jnp.sum(sc, axis=1, keepdims=True) * (1.0 / C)
    m2 = jnp.sum(sc * nraw, axis=1, keepdims=True) * (1.0 / C)
    dc = (inv * (sc - m1 - nraw * m2)).astype(BF16)
    vacc[4] += part(dc.astype(F32))
    dcv[pl.ds(2 * s, 2)] = dc.reshape(2, ROWS, C)


def peers_of(me, coord, stride):
    return [me + (lax.rem(coord + o, 4) - coord) * stride for o in (1, 2, 3)]


def send(src, dst, sems, idx, dev):
    copy = pltpu.make_async_remote_copy(
        src_ref=src, dst_ref=dst, send_sem=sems[0].at[idx], recv_sem=sems[1].at[idx],
        device_id=(dev,), device_id_type=MESH)
    copy.start()
    return copy


def wait_all(copies):
    for copy in copies:
        copy.wait()


def kernel(widths, feat, cot, s1, s2, taps, vecs_ref,
           d_out, small_out, o1_out, o2_out,
           xsend, xmate, hsend, xhalo, csend, cmate,
           bx1, bx2, w1g, w2g, xf, df, tapb, tapf, conv, cotb, w1, w2, w1c, g1, g2, vacc, dcv,
           g1b, g2b, dsend, dhalo, rc1, rc2, c1, c2, rz1, ry2, t1, t2, ry1, rz2, p1, p2, rx1, rx2,
           kacc, cur, slots, dimg, rsend, rmate, ssem, rsem):
    me = lax.axis_index("strip")
    core = lax.rem(me, 2)
    y = lax.rem(me // 2, 4)
    x = lax.rem(me // 8, 4)
    z = me // 32
    xs, ys, zs = peers_of(me, x, 8), peers_of(me, y, 2), peers_of(me, z, 32)
    mate = me + 1 - 2 * core
    outer = lax.rem(me + 2 * core - 1 + N_DEV, N_DEV)
    sems = (ssem, rsem)
    is_a = core == 0
    wa, wb = widths[me - core], widths[me - core + 1]
    pair = wa + wb
    n0 = (pair + 1) // 2
    n = jnp.where(is_a, n0, pair - n0)
    p0 = jnp.where(is_a, 0, n0)
    mine = jnp.where(is_a, wa, wb)
    base = jnp.where(is_a, 0, wa)
    off9 = jnp.maximum(wa - 9, 0)
    off6 = jnp.maximum(wa - 6, 0)
    offr = jnp.maximum(n0 - 6, 0)

    barrier = pltpu.get_barrier_semaphore()
    for dev in xs + ys + zs + [mate, outer]:
        pl.semaphore_signal(barrier, inc=1, device_id=(dev,), device_id_type=MESH)

    s9, s6 = jnp.where(is_a, off9, 0), jnp.where(is_a, off6, 0)
    for i in range(9):
        xsend[i] = feat[s9 + i]
    for i in range(6):
        csend[i] = cot[s6 + i]
    h3 = jnp.where(is_a, 0, jnp.maximum(wb - 3, 0))
    for i in range(3):
        hsend[i] = feat[h3 + i]
    pl.semaphore_wait(barrier, 11)

    halo_in = [send(hsend, xhalo, sems, 0, outer), send(xsend, xmate, sems, 1, mate)]
    first = []
    for o in range(3):
        first.append(send(s1, bx1.at[x], sems, 2 + o, xs[o]))
        first.append(send(s2, bx2.at[x], sems, 5 + o, xs[o]))
    cot_in = send(csend, cmate, sems, 8, mate)
    bx1[x] = s1[...]
    bx2[x] = s2[...]
    fill_taps(taps, tapb, False)
    clear_pads(xf)
    clear_pads(df)
    wait_all(first)
    w1g[core, z, y] = jnp.concatenate([bx1[q].astype(F32)[:12] for q in range(4)], axis=0).astype(BF16)
    w2g[core, z, y] = jnp.concatenate([bx2[q].astype(F32)[:12] for q in range(4)], axis=0).astype(BF16)
    second = []
    for o in range(3):
        second.append(send(w1g.at[core, z, y], w1g.at[core, z, y], sems, 9 + o, ys[o]))
        second.append(send(w2g.at[core, z, y], w2g.at[core, z, y], sems, 12 + o, zs[o]))
    wait_all(halo_in)

    def place_x(i, _):
        p = p0 + i - 3
        q = p - base
        own = feat[jnp.clip(q, 0, CAP - 1)].astype(F32)
        other = xmate[jnp.clip(jnp.where(is_a, p - wa, p - off9), 0, 8)].astype(F32)
        edge = xhalo[jnp.clip(jnp.where(is_a, p + 3, p - pair), 0, 2)].astype(F32)
        is_own = (q >= 0) & (q < mine)
        is_edge = jnp.where(is_a, p < 0, p >= pair)
        gone = (i >= n + 6) | (is_edge & jnp.where(is_a, me == 0, me == N_DEV - 1))
        val = jnp.where(is_own, own, jnp.where(is_edge, edge, other))
        put_column(xf, i, jnp.where(gone, 0.0, val))
        return 0
    lax.fori_loop(0, XC, place_x, 0)
    wait_all(second)
    third = []
    for o in range(3):
        third.append(send(w1g.at[core, z], w1g.at[core, z], sems, 15 + o, zs[o]))
        third.append(send(w2g.at[core, :, y], w2g.at[core, :, y], sems, 18 + o, ys[o]))
    conv_block(xf, tapb, conv, 0)
    cot_in.wait()

    def place_cot(j, _):
        p = p0 + j
        q = p - base
        own = cot[jnp.clip(q, 0, CAP - 1)].astype(F32)
        other = cmate[jnp.clip(jnp.where(is_a, p - wa, p - off6), 0, 5)].astype(F32)
        val = jnp.where((q >= 0) & (q < mine), own, other)
        cotb[j] = jnp.where(j >= n, 0.0, val).astype(BF16)
        return 0
    lax.fori_loop(0, NC, place_cot, 0)
    conv_block(xf, tapb, conv, 1)
    wait_all(third)
    fourth = [send(w1g.at[core], w1g.at[core], sems, 21, mate), send(w2g.at[core], w2g.at[core], sems, 22, mate)]
    conv_block(xf, tapb, conv, 2)
    fill_taps(taps, tapf, True)
    vacc[...] = jnp.zeros_like(vacc)
    g1[...] = jnp.zeros_like(g1)
    g2[...] = jnp.zeros_like(g2)
    wait_all(fourth)

    w1full = w1g[...].reshape(FF, 512)
    w2full = w2g[...].reshape(FF, C)
    for f in range(FF // 256):
        sl = slice(f * 256, f * 256 + 256)
        w1[:, sl] = w1full[sl].T
        w2[:, sl] = w2full[sl].T
        w1c[f] = w1full[sl, :C]
    vecs = (vecs_ref[0:1, :], vecs_ref[1:2, :], vecs_ref[2:3, :], vecs_ref[3:4, :])

    def step(s, _):
        mlp_step(s, conv, cotb, vecs, w1, w2, w1c, g1, g2, vacc, dcv)
        return 0
    lax.fori_loop(0, NC // 2, step, 0)

    last_at = jnp.maximum(n - 3, 0)
    inner_at, outer_at = jnp.where(is_a, last_at, 0), jnp.where(is_a, 0, last_at)
    for i in range(3):
        dsend[0, i] = dcv[inner_at + i]
        dsend[1, i] = dcv[outer_at + i]
    halo_d = [send(dsend.at[0], dhalo.at[0], sems, 23, mate), send(dsend.at[1], dhalo.at[1], sems, 24, outer)]
    srow = jnp.zeros((8, C), F32)
    for q in range(4):
        b1 = g1[:, q * 384:(q + 1) * 384].T
        b2 = g2[:, q * 384:(q + 1) * 384].T
        srow += (b2 * w2full[q * 384:(q + 1) * 384].astype(F32)).reshape(48, 8, C).sum(0)
        for k in range(8):
            at = (q // 2, (q % 2) * 2 + k // 4, k % 4)
            g1b[at] = b1[k * 48:(k + 1) * 48].astype(BF16)
            g2b[at] = b2[k * 48:(k + 1) * 48].astype(BF16)
    vacc[3] = srow
    rs1 = [send(g1b.at[1 - core], rc1, sems, 25, mate), send(g2b.at[1 - core], rc2, sems, 26, mate)]

    def place_d(j, _):
        put_column(df, j + 3, dcv[j])
        return 0
    lax.fori_loop(0, NC, place_d, 0)
    kernel_grads(xf, df, kacc, 0)
    wait_all(rs1)

    def add_first(i, _):
        zi, yi = i // 4, lax.rem(i, 4)
        c1[zi, yi] = (g1b[core, zi, yi].astype(F32) + rc1[zi, yi].astype(F32)).astype(BF16)
        c2[zi, yi] = (g2b[core, zi, yi].astype(F32) + rc2[zi, yi].astype(F32)).astype(BF16)
        return 0
    lax.fori_loop(0, 16, add_first, 0)
    rs2 = []
    for o in range(3):
        rs2.append(send(c1.at[lax.rem(z + o + 1, 4)], rz1.at[o], sems, 27 + o, zs[o]))
        rs2.append(send(c2.at[:, lax.rem(y + o + 1, 4)], ry2.at[o], sems, 30 + o, ys[o]))
    kernel_grads(xf, df, kacc, 1)
    kernel_grads(xf, df, kacc, 2)

    def kout(i, _):
        cur[0, pl.ds(i, 1), :] = jnp.concatenate([jnp.sum(kacc[i, g], axis=0, keepdims=True) for g in range(3)], axis=1)
        return 0
    lax.fori_loop(0, 49, kout, 0)
    rows = [jnp.sum(vacc[i], axis=0, keepdims=True) for i in range(5)]
    cur[0, 49:56, :] = jnp.zeros((7, C), F32)
    cur[0, 56:64, :] = jnp.concatenate(rows + [jnp.zeros((3, C), F32)], axis=0)

    def sum_send(stage, at, group):
        return [send(cur.at[stage], slots.at[at + i], sems, 49 + at + i, dev) for i, dev in enumerate(group)]

    def sum_take(stage, at, copies):
        wait_all(copies)
        total = cur[stage]
        for i in range(len(copies)):
            total = total + slots[at + i]
        cur[stage + 1] = total

    sums = sum_send(0, 0, [mate])
    wait_all(halo_d)

    def place_edges(i, _):
        k = jnp.clip(i - n - 3, 0, 2)
        left = jnp.where(is_a, dhalo[1, jnp.clip(i, 0, 2)].astype(F32), dhalo[0, jnp.clip(i, 0, 2)].astype(F32))
        right = jnp.where(is_a, dhalo[0, k].astype(F32), dhalo[1, k].astype(F32))
        left = jnp.where(me == 0, 0.0, left)
        right = jnp.where((i >= n + 6) | (me == N_DEV - 1), 0.0, right)
        own = dcv[jnp.clip(i - 3, 0, NC - 1)].astype(F32)
        put_column(df, i, jnp.where(i < 3, left, jnp.where(i < n + 3, own, right)))
        return 0
    lax.fori_loop(0, XC, place_edges, 0)
    sum_take(0, 0, sums)
    sums = sum_send(1, 1, ys)
    back_block(df, tapf, cotb, dimg, 0)
    wait_all(rs2)

    def add_second(i, _):
        t1[i] = (c1[z, i].astype(F32) + rz1[0, i].astype(F32) + rz1[1, i].astype(F32) + rz1[2, i].astype(F32)).astype(BF16)
        t2[i] = (c2[i, y].astype(F32) + ry2[0, i].astype(F32) + ry2[1, i].astype(F32) + ry2[2, i].astype(F32)).astype(BF16)
        return 0
    lax.fori_loop(0, 4, add_second, 0)
    rs3 = []
    for o in range(3):
        rs3.append(send(t1.at[lax.rem(y + o + 1, 4)], ry1.at[o], sems, 33 + o, ys[o]))
        rs3.append(send(t2.at[lax.rem(z + o + 1, 4)], rz2.at[o], sems, 36 + o, zs[o]))
    sum_take(1, 1, sums)
    sums = sum_send(2, 4, zs)
    back_block(df, tapf, cotb, dimg, 1)
    wait_all(rs3)
    u1 = t1[y].astype(F32) + ry1[0].astype(F32) + ry1[1].astype(F32) + ry1[2].astype(F32)
    u2 = t2[z].astype(F32) + rz2[0].astype(F32) + rz2[1].astype(F32) + rz2[2].astype(F32)
    for q in range(4):
        p1[q, 0:12, :] = u1[q * 12:q * 12 + 12]
        p2[q, 0:12, :] = u2[q * 12:q * 12 + 12]
        p1[q, 12:16, :] = jnp.zeros((4, 512), F32)
        p2[q, 12:16, :] = jnp.zeros((4, C), F32)
    rs4 = []
    for o in range(3):
        q = lax.rem(x + o + 1, 4)
        rs4.append(send(p1.at[q], rx1.at[o], sems, 39 + o, xs[o]))
        rs4.append(send(p2.at[q], rx2.at[o], sems, 42 + o, xs[o]))
    sum_take(2, 4, sums)
    sums = sum_send(3, 7, xs)
    back_block(df, tapf, cotb, dimg, 2)
    sr = jnp.where(is_a, offr, 0)
    for i in range(6):
        rsend[i] = dimg[sr + i]
    back = send(rsend, rmate, sems, 45, mate)
    wait_all(rs4)
    o1_out[...] = (p1[x] + rx1[0] + rx1[1] + rx1[2]) * SCALE
    o2_out[...] = (p2[x] + rx2[0] + rx2[1] + rx2[2]) * SCALE
    sum_take(3, 7, sums)
    small_out[...] = cur[4] * SCALE
    back.wait()

    def place_out(s, _):
        p = base + s
        own = dimg[jnp.clip(p - p0, 0, NC - 1)]
        other = rmate[jnp.clip(jnp.where(is_a, p - n0, p - offr), 0, 5)]
        is_own = jnp.where(is_a, p < n0, p >= n0)
        val = jnp.where(is_own, own.astype(F32), other.astype(F32))
        d_out[s] = jnp.where(s >= mine, 0.0, val).astype(BF16)
        return 0
    lax.fori_loop(0, CAP, place_out, 0)


def fused(widths, feat, cot, s1, s2, taps, vecs):
    def v(*shape, dtype=BF16):
        return pltpu.VMEM(shape, dtype)
    return pl.pallas_call(
        kernel,
        out_shape=(
            jax.ShapeDtypeStruct((CAP, ROWS, C), BF16),
            jax.ShapeDtypeStruct((64, C), F32),
            jax.ShapeDtypeStruct((16, 512), F32),
            jax.ShapeDtypeStruct((16, C), F32),
        ),
        in_specs=[SMEM] + [VMEM] * 6,
        out_specs=[VMEM] * 4,
        scratch_shapes=[
            v(9, ROWS, C), v(9, ROWS, C), v(3, ROWS, C), v(3, ROWS, C), v(6, ROWS, C), v(6, ROWS, C),
            v(4, 16, 512), v(4, 16, C), v(2, 4, 4, 48, 512), v(2, 4, 4, 48, C),
            v(XC, 3, RP, 128, dtype=F32), v(XC, 3, RP, 128, dtype=F32),
            v(49, 3, 8, 128, dtype=F32), v(49, 3, 8, 128, dtype=F32),
            v(NC, 3, ROWS, 128, dtype=F32), v(NC, ROWS, C),
            v(512, FF), v(C, FF), v(FF // 256, 256, C), v(512, FF, dtype=F32), v(C, FF, dtype=F32),
            v(8, 8, C, dtype=F32), v(NC, ROWS, C),
            v(2, 4, 4, 48, 512), v(2, 4, 4, 48, C), v(2, 3, ROWS, C), v(2, 3, ROWS, C),
            v(4, 4, 48, 512), v(4, 4, 48, C), v(4, 4, 48, 512), v(4, 4, 48, C),
            v(3, 4, 48, 512), v(3, 4, 48, C), v(4, 48, 512), v(4, 48, C), v(3, 48, 512), v(3, 48, C),
            v(4, 16, 512, dtype=F32), v(4, 16, C, dtype=F32), v(3, 16, 512, dtype=F32), v(3, 16, C, dtype=F32),
            v(49, 3, 8, 128, dtype=F32), v(5, 64, C, dtype=F32), v(10, 64, C, dtype=F32),
            v(NC, ROWS, C), v(6, ROWS, C), v(6, ROWS, C),
            pltpu.SemaphoreType.DMA((59,)), pltpu.SemaphoreType.DMA((59,)),
        ],
        compiler_params=pltpu.CompilerParams(collective_id=0, has_side_effects=True, vmem_limit_bytes=60 * 2**20),
        name="block_back",
    )(widths, feat, cot, s1, s2, taps, vecs)


def local(features, grad_out, widths, dw_kernel, dw_bias, ln_gain, ln_bias,
          w_in, in_bias, w_out, out_bias, layer_scale):
    feat, cot = jnp.transpose(features, (1, 0, 2)), jnp.transpose(grad_out, (1, 0, 2))
    s1 = jnp.pad(jnp.concatenate([w_in.T, in_bias[:, None]], axis=1), ((0, 4), (0, 127)))
    s2 = jnp.pad(w_out, ((0, 4), (0, 0)))
    vecs = jnp.concatenate([dw_bias, ln_gain, ln_bias, layer_scale]).reshape(4, C).astype(F32)
    dimg, total, o1, o2 = fused(widths, feat, cot, s1, s2, dw_kernel, vecs)
    g_scale = (total[59] + out_bias.astype(F32) * total[58]) / layer_scale.astype(F32)
    return (jnp.transpose(dimg, (1, 0, 2)), total[:49], total[60], total[56], total[57],
            o1[:12, :C].T, o1[:12, C], o2[:12], total[58], g_scale)


def solution(mesh):
    wide = P(None, "strip", None)
    return jax.shard_map(
        local, mesh=mesh,
        in_specs=(wide, wide, P(), P(), P(), P(), P(), P(None, "strip"), P("strip"), P("strip", None), P(), P()),
        out_specs=(wide, P(), P(), P(), P(), P(None, "strip"), P("strip"), P("strip", None), P(), P()),
        check_vma=False)
```

time: 1240 us -> 114 us (0.09); the launches traced: 1230 us -> 114 us
  blocking collectives: 476 us -> 0 us
  other arithmetic: 354 us -> 2.66 us
  starting transfers between devices: 186 us -> 0 us
  Pallas kernels: 0 us -> 99 us
  waiting for transfers between devices: 73.9 us -> 0 us
  local copies, waits for them, and re-layouts: 74.9 us -> 11.7 us
  matrix products: 43 us -> 0 us
  between operations: 19.7 us -> 0.66 us
    unnamed x2 -> x0, blocking collectives: 414 us -> none
    reduce_sum x8 -> x0, other arithmetic: 211 us -> none  [the longest x1 115 us: mlp_back(): mean_val = jnp.mean(values, axis=-1, keepdims=True)]
    unnamed x64 -> x0, starting transfers between devices: 175 us -> none
    convert_element_type x11 -> x1, other arithmetic: 130 us -> 0.74 us  [local(): jnp.concatenate([dw_bias, ln_gain, ln_bias, layer_scale]).reshape(4, C)]
    pallas_call x0 -> x1, Pallas kernels: none -> 99 us  [fused(): pl.pallas_call(kernel, out_shape=(jax.ShapeDtypeStruct((CAP, ROWS, C), BF...]
    psum x1 -> x0, waiting for transfers between devices: 73 us -> none  [local(): lax.psum((g_kernel, g_dwbias, g_lgain, g_lbias, g_obias, g_scale), 'strip')]
    psum x1 -> x0, blocking collectives: 62 us -> none  [local(): lax.psum((g_kernel, g_dwbias, g_lgain, g_lbias, g_obias, g_scale), 'strip')]
    dot_general x6 -> x0, matrix products: 43 us -> none  [the longest x1 10.2 us: mlp_back(): lax.dot_general(d_mlp, w_out, (((1,), (1,)), ((), ())), preferred_element...]
  transfers between devices with their start and end apart: 71 -> 0, of which waited for: 1 -> 0; matrix products, arithmetic and copies ran while one was open for 26% -> 0% of each run, Pallas kernels for 0% -> 0%
where the time goes in v2:
time: 114 us
  Pallas kernels  99 us (87%)
  local copies, waits for them, and re-layouts  11.7 us (10%)
  other arithmetic  2.66 us (2%)
    pallas_call x1, Pallas kernels, fused(): pl.pallas_call(kernel, out_shape=(jax.ShapeDtypeStruct((CAP, ROWS, C), BF...  99 us
    unnamed x10, local copies, waits for them, and re-layouts  3.31 us

profile of v2, /device:TPU:1, one launch (start us, length us, event | category | flops | bytes accessed | tf_op | source)
XLA Modules:
  0.0 114.0 jit_solution(10354468584643128789)
XLA Ops:
  0.6 0.7 copy.23
  1.4 1.3 %fusion.5.s1 = bf16[16,512]{1,0:T(8,128)(2,1)} fusion(bf16[12,1]{1,0:T(8,128)(2,1)S(1)} %copy.23, bf16[12,384]{1,0:T(8,128)(2,1)} %bitcast.12), kind=kLoop, calls=%fused_computation.8 | loop fusion | flops 90112 | bytes 25624 | tf_op jit(solution)/shard_map/concatenate | solution.py:454
  2.7 0.7 maximum_convert_fusion
  3.5 0.6 reshape.23.vecs_ref
  4.1 1.3 %pad.9.s2 = bf16[16,384]{1,0:T(8,128)(2,1)} pad(bf16[12,384]{1,0:T(8,128)(2,1)} %param.21, bf16[]{:T(256)} %constant.2.clone.1), padding=0_4x0_0 | pad | bytes 21506 | tf_op jit(solution)/shard_map/jit(_pad)/pad | solution.py:455
  5.4 0.0 copy-start.2
  5.4 0.0 copy-start.3
  5.4 99.0 %block_back.1 = (bf16[15,128,384]{2,1,0:T(8,128)(2,1)}, f32[64,384]{1,0:T(8,128)}, f32[16,512]{1,0:T(8,128)}, f32[16,384]{1,0:T(8,128)}) custom-call(s32[128]{0:T(128)} %widths.1, bf16[15,128,384]{2,1,0:T(8,128)(2,1)} %bitcast.8, bf16[15,128,384]{2,1,0:T(8,128)(2,1)} %bitcast.9, bf16[16,512]{1,0:T(8,128)(2,1)} %fusion.5.s1, bf16[16,384]{1,0:T(8,128)(2,1)} %pad.9.s2, ...), custom_call_target="tpu_custom_call" | custom-call | tf_op jit(solution)/shard_map/block_back/pallas_call | solution.py:420
  104.3 1.5 %slice_reduce_fusion.1 = (f32[384]{0:T(512)S(1)}, f32[384]{0:T(512)S(1)}, f32[384]{0:T(512)}, f32[384]{0:T(512)}, f32[384]{0:T(512)}) fusion(f32[64,384]{1,0:T(8,128)} %get-tuple-element.15), kind=kLoop, calls=%fused_computation.12 | loop fusion | bytes 15360 | tf_op jit(solution)/shard_map/slice | solution.py:458
  105.9 0.0 copy-start.1
  105.9 0.0 copy-done.2
  105.9 0.0 copy-done.3
  105.9 0.6 convert_divide_fusion
  106.4 1.5 %slice.28 = f32[49,384]{1,0:T(8,128)} slice(f32[64,384]{1,0:T(8,128)} %get-tuple-element.15), slice={[0:49], [0:384]} | slice | bytes 150528 | tf_op jit(solution)/shard_map/slice | solution.py:459
  108.0 1.3 %slice_bitcast_fusion = f32[384,12]{0,1:T(8,128)} fusion(f32[16,512]{1,0:T(8,128)} %get-tuple-element.16), kind=kLoop, calls=%fused_computation.7 | loop fusion | bytes 36864 | tf_op jit(solution)/shard_map/transpose | solution.py:460
  109.3 1.3 %slice_reduce_fusion = f32[12]{0:T(128)} fusion(f32[16,512]{1,0:T(8,128)} %get-tuple-element.16), kind=kLoop, calls=%fused_computation.9 | loop fusion | bytes 96 | tf_op jit(solution)/shard_map/slice | solution.py:460
  110.6 0.0 copy-start
  110.6 2.7 %copy.26 = bf16[128,15,384]{2,0,1:T(8,128)(2,1)} copy(bf16[128,15,384]{2,0,1:T(8,128)(2,1)} %bitcast.10) | data formatting | bytes 2949120
  113.3 0.0 copy-done.1
  113.3 0.0 copy-done
  113.3 0.6 copy.27
Async XLA Ops:
  5.4 100.5 %copy-start.2 = (bf16[384]{0:T(512)(128)(2,1)S(1)}, bf16[384]{0:T(512)(128)(2,1)}, u32[]{:S(2)}) copy-start(bf16[384]{0:T(512)(128)(2,1)} %param.23) | copy-start | bytes 2308
  5.4 100.5 %copy-start.3 = (bf16[384]{0:T(512)(128)(2,1)S(1)}, bf16[384]{0:T(512)(128)(2,1)}, u32[]{:S(2)}) copy-start(bf16[384]{0:T(512)(128)(2,1)} %param.22) | copy-start | bytes 2308
  105.9 7.5 %copy-start.1 = (f32[384]{0:T(512)}, f32[384]{0:T(512)S(1)}, u32[]{:S(2)}) copy-start(f32[384]{0:T(512)S(1)} %get-tuple-element.41) | copy-start | bytes 4612
  110.6 2.7 %copy-start = (f32[16,384]{1,0:T(8,128)S(1)}, f32[16,384]{1,0:T(8,128)}, u32[]{:S(2)}) copy-start(f32[16,384]{1,0:T(8,128)} %get-tuple-element.17) | copy-start | bytes 73732

commit v3 on v2

--- a/solution.py
+++ b/solution.py
@@ -10,9 +10,9 @@
 ROWS, C, FF, CAP = 128, 384, 1536, 15
 N_DEV = 128
 NC = 12
+NW = 11
 XC = NC + 6
 RP = ROWS + 16
-J = 4
 T = 2 * ROWS
 F32, BF16 = jnp.float32, jnp.bfloat16
 VMEM = pl.BlockSpec(memory_space=pltpu.VMEM)
@@ -56,63 +56,57 @@
     lax.fori_loop(0, XC, body, 0)
 
 
-def conv_cols(xf, tapb, g, j0, r0):
-    accs = [None] * J
-    for a in range(7):
-        xs = [xf[j0 + i, g, pl.ds(r0 + 5 + a, 8), :] for i in range(J + 6)]
-        for b in range(7):
-            t = tapb[a * 7 + b, g]
-            for j in range(J):
-                p = t * xs[j + b]
-                accs[j] = p if accs[j] is None else accs[j] + p
-    return accs
-
-
-def conv_block(xf, tapb, conv, jb):
-    def gloop(g, _):
-        def rloop(r, _):
-            r0 = r * 8
-            accs = conv_cols(xf, tapb, g, jb * J, r0)
-            for j in range(J):
-                conv[jb * J + j, g, pl.ds(pl.multiple_of(r0, 8), 8), :] = accs[j]
-            return 0
-        lax.fori_loop(0, 16, rloop, 0)
-        return 0
-    lax.fori_loop(0, 3, gloop, 0)
-
-
-def back_block(df, tapb, cotb, dimg, jb):
-    for g in range(3):
-        ls = slice(g * 128, g * 128 + 128)
-
-        def rloop(r, _):
-            r0 = pl.multiple_of(r * 16, 16)
-            lo = conv_cols(df, tapb, g, jb * J, r0)
-            hi = conv_cols(df, tapb, g, jb * J, r0 + 8)
-            for j in range(J):
-                col = jb * J + j
-                acc = jnp.concatenate([lo[j], hi[j]], axis=0) + cotb[col, pl.ds(r0, 16), ls].astype(F32)
-                dimg[col, pl.ds(r0, 16), ls] = acc.astype(BF16)
-            return 0
-        lax.fori_loop(0, 8, rloop, 0)
+def conv_rows(xf, tapb, g, r0):
+    def aloop(a, accs):
+        accs = [list(part_) for part_ in accs]
+        ts = [tapb[a * 7 + b, g] for b in range(7)]
+        for i in range(NW + 6):
+            for k in range(2):
+                xv = xf[i, g, pl.ds(r0 + 8 * k + 5 + a, 8), :]
+                for b in range(7):
+                    if 0 <= i - b < NW:
+                        accs[k][i - b] = accs[k][i - b] + ts[b] * xv
+        return tuple(tuple(part_) for part_ in accs)
+    zero = jnp.zeros((8, 128), F32)
+    return lax.fori_loop(0, 7, aloop, ((zero,) * NW,) * 2)
+
+
+def conv_group(xf, tapb, conv, g):
+    def rloop(r, _):
+        r0 = pl.multiple_of(r * 16, 16)
+        lo, hi = conv_rows(xf, tapb, g, r0)
+        for j in range(NW):
+            conv[j, g, pl.ds(r0, 16), :] = jnp.concatenate([lo[j], hi[j]], axis=0)
+        return 0
+    lax.fori_loop(0, 8, rloop, 0)
+
+
+def back_group(df, tapb, cotb, dimg, g):
+    ls = slice(g * 128, g * 128 + 128)
+
+    def rloop(r, _):
+        r0 = pl.multiple_of(r * 16, 16)
+        lo, hi = conv_rows(df, tapb, g, r0)
+        for j in range(NW):
+            acc = jnp.concatenate([lo[j], hi[j]], axis=0) + cotb[j, pl.ds(r0, 16), ls].astype(F32)
+            dimg[j, pl.ds(r0, 16), ls] = acc.astype(BF16)
+        return 0
+    lax.fori_loop(0, 8, rloop, 0)
 
 
 def kernel_grads(xf, df, kacc, g):
     def aloop(a, _):
-        def jloop(jb, accs):
-            def rloop(r, accs):
-                r0 = r * 8
-                accs = list(accs)
-                ds = [df[jb * J + 3 + j, g, pl.ds(pl.multiple_of(r0 + 8, 8), 8), :] for j in range(J)]
-                xs = [xf[jb * J + i, g, pl.ds(r0 + 5 + a, 8), :] for i in range(J + 6)]
+        def rloop(r, accs):
+            r0 = r * 8
+            accs = list(accs)
+            ds = [df[3 + j, g, pl.ds(pl.multiple_of(r0 + 8, 8), 8), :] for j in range(NW)]
+            for i in range(NW + 6):
+                xv = xf[i, g, pl.ds(r0 + 5 + a, 8), :]
                 for b in range(7):
-                    p = ds[0] * xs[b]
-                    for j in range(1, J):
-                        p = p + ds[j] * xs[j + b]
-                    accs[b] = accs[b] + p
-                return tuple(accs)
-            return lax.fori_loop(0, 16, rloop, accs, unroll=4)
-        accs = lax.fori_loop(0, NC // J, jloop, tuple(jnp.zeros((8, 128), F32) for _ in range(7)))
+                    if 0 <= i - b < NW:
+                        accs[b] = accs[b] + ds[i - b] * xv
+            return tuple(accs)
+        accs = lax.fori_loop(0, 16, rloop, tuple(jnp.zeros((8, 128), F32) for _ in range(7)), unroll=2)
         for b in range(7):
             kacc[a * 7 + b, g] = accs[b]
         return 0
@@ -137,17 +131,24 @@
     vacc[2] += part(dmlp.astype(F32))
     normed_t = normed.T
     dmlp_t = dmlp.T
-    dn = jnp.zeros((T, C), F32)
-    for f in range(FF // 256):
-        sl = slice(f * 256, f * 256 + 256)
-        pre = jnp.dot(normed, w1[:, sl], preferred_element_type=F32)
-        dact = jnp.dot(dmlp, w2[:, sl], preferred_element_type=F32)
+    blocks = [slice(f * 256, f * 256 + 256) for f in range(FF // 256)]
+
+    def front(sl):
+        return (jnp.dot(normed, w1[:, sl], preferred_element_type=F32),
+                jnp.dot(dmlp, w2[:, sl], preferred_element_type=F32))
+    acts, dpres = [], []
+    ahead = front(blocks[0])
+    for f in range(len(blocks)):
+        pre, dact = ahead
+        if f + 1 < len(blocks):
+            ahead = front(blocks[f + 1])
         act, slope = gelu_parts(pre)
-        act = act.astype(BF16)
-        dpre = (dact * slope).astype(BF16)
+        acts.append(act.astype(BF16))
+        dpres.append((dact * slope).astype(BF16))
+    dn = jnp.dot(jnp.concatenate(dpres, axis=1), w1t[...], preferred_element_type=F32)
+    for sl, act, dpre in zip(blocks, acts, dpres):
         g1[:, sl] += jnp.dot(normed_t, dpre, preferred_element_type=F32)
         g2[:, sl] += jnp.dot(dmlp_t, act, preferred_element_type=F32)
-        dn += jnp.dot(dpre, w1t[f], preferred_element_type=F32)
     vacc[0] += part(dn * nraw)
     vacc[1] += part(dn)
     sc = dn * gain
@@ -175,12 +176,13 @@
         copy.wait()
 
 
-def kernel(widths, feat, cot, s1, s2, taps, vecs_ref,
-           d_out, small_out, o1_out, o2_out,
+def kernel(widths, feat, cot, w_in_t, in_bias, w_out, taps, dw_bias, ln_gain, ln_bias, layer_scale,
+           dimg_out, rmate_out, small_out, o1_out, o2_out,
+           s1, s2, sbias,
            xsend, xmate, hsend, xhalo, csend, cmate,
            bx1, bx2, w1g, w2g, xf, df, tapb, tapf, conv, cotb, w1, w2, w1c, g1, g2, vacc, dcv,
            g1b, g2b, dsend, dhalo, rc1, rc2, c1, c2, rz1, ry2, t1, t2, ry1, rz2, p1, p2, rx1, rx2,
-           kacc, cur, slots, dimg, rsend, rmate, ssem, rsem):
+           kacc, krow, cur, mslot, part_sum, slots, total, dimg, rsend, rmate, ssem, rsem):
     me = lax.axis_index("strip")
     core = lax.rem(me, 2)
     y = lax.rem(me // 2, 4)
@@ -214,6 +216,12 @@
     h3 = jnp.where(is_a, 0, jnp.maximum(wb - 3, 0))
     for i in range(3):
         hsend[i] = feat[h3 + i]
+    sbias[...] = jnp.zeros_like(sbias)
+    sbias[0:1, 0:12] = in_bias[...].astype(F32).reshape(1, 12)
+    s1[:, C:512] = sbias[...].T[0:16].astype(BF16)
+    pad4 = jnp.zeros((4, C), F32)
+    s1[:, 0:C] = jnp.concatenate([w_in_t[...].astype(F32), pad4], axis=0).astype(BF16)
+    s2[...] = jnp.concatenate([w_out[...].astype(F32), pad4], axis=0).astype(BF16)
     pl.semaphore_wait(barrier, 11)
 
     halo_in = [send(hsend, xhalo, sems, 0, outer), send(xsend, xmate, sems, 1, mate)]
@@ -250,11 +258,13 @@
         return 0
     lax.fori_loop(0, XC, place_x, 0)
     wait_all(second)
-    third = []
-    for o in range(3):
-        third.append(send(w1g.at[core, z], w1g.at[core, z], sems, 15 + o, zs[o]))
-        third.append(send(w2g.at[core, :, y], w2g.at[core, :, y], sems, 18 + o, ys[o]))
-    conv_block(xf, tapb, conv, 0)
+    third1, third2 = [], []
+    for o in range(3):
+        third1.append(send(w1g.at[core, z], w1g.at[core, z], sems, 15 + o, zs[o]))
+        third2.append(send(w2g.at[core, :, y], w2g.at[core, :, y], sems, 18 + o, ys[o]))
+    fourth = [send(w1g.at[core, z], w1g.at[core, z], sems, 21, mate),
+              send(w2g.at[core, :, y], w2g.at[core, :, y], sems, 22, mate)]
+    conv_group(xf, tapb, conv, 0)
     cot_in.wait()
 
     def place_cot(j, _):
@@ -266,24 +276,28 @@
         cotb[j] = jnp.where(j >= n, 0.0, val).astype(BF16)
         return 0
     lax.fori_loop(0, NC, place_cot, 0)
-    conv_block(xf, tapb, conv, 1)
-    wait_all(third)
-    fourth = [send(w1g.at[core], w1g.at[core], sems, 21, mate), send(w2g.at[core], w2g.at[core], sems, 22, mate)]
-    conv_block(xf, tapb, conv, 2)
+    conv_group(xf, tapb, conv, 1)
+    for o in range(3):
+        zb, yb = lax.rem(z + 3 - o, 4), lax.rem(y + 3 - o, 4)
+        third1[o].wait()
+        fourth.append(send(w1g.at[core, zb], w1g.at[core, zb], sems, 59 + o, mate))
+        third2[o].wait()
+        fourth.append(send(w2g.at[core, :, yb], w2g.at[core, :, yb], sems, 62 + o, mate))
+    conv_group(xf, tapb, conv, 2)
+    conv[NC - 1] = jnp.zeros((3, ROWS, 128), F32)
     fill_taps(taps, tapf, True)
     vacc[...] = jnp.zeros_like(vacc)
     g1[...] = jnp.zeros_like(g1)
     g2[...] = jnp.zeros_like(g2)
     wait_all(fourth)
-
     w1full = w1g[...].reshape(FF, 512)
     w2full = w2g[...].reshape(FF, C)
     for f in range(FF // 256):
         sl = slice(f * 256, f * 256 + 256)
         w1[:, sl] = w1full[sl].T
         w2[:, sl] = w2full[sl].T
-        w1c[f] = w1full[sl, :C]
-    vecs = (vecs_ref[0:1, :], vecs_ref[1:2, :], vecs_ref[2:3, :], vecs_ref[3:4, :])
+        w1c[sl, :] = w1full[sl, :C]
+    vecs = tuple(ref[...].astype(F32).reshape(1, C) for ref in (dw_bias, ln_gain, ln_bias, layer_scale))
 
     def step(s, _):
         mlp_step(s, conv, cotb, vecs, w1, w2, w1c, g1, g2, vacc, dcv)
@@ -297,16 +311,21 @@
         dsend[1, i] = dcv[outer_at + i]
     halo_d = [send(dsend.at[0], dhalo.at[0], sems, 23, mate), send(dsend.at[1], dhalo.at[1], sems, 24, outer)]
     srow = jnp.zeros((8, C), F32)
-    for q in range(4):
-        b1 = g1[:, q * 384:(q + 1) * 384].T
-        b2 = g2[:, q * 384:(q + 1) * 384].T
-        srow += (b2 * w2full[q * 384:(q + 1) * 384].astype(F32)).reshape(48, 8, C).sum(0)
-        for k in range(8):
-            at = (q // 2, (q % 2) * 2 + k // 4, k % 4)
-            g1b[at] = b1[k * 48:(k + 1) * 48].astype(BF16)
-            g2b[at] = b2[k * 48:(k + 1) * 48].astype(BF16)
+    rs1 = []
+    for h in range(2):
+        half = 1 - core if h == 0 else core
+        for q in range(2):
+            at = pl.ds(pl.multiple_of(half * 768 + q * 384, 128), 384)
+            b1 = g1[:, at].T
+            b2 = g2[:, at].T
+            wrow = w2g[half, pl.ds(2 * q, 2)].reshape(384, C)
+            srow += (b2 * wrow.astype(F32)).reshape(48, 8, C).sum(0)
+            for k in range(8):
+                g1b[half, 2 * q + k // 4, k % 4] = b1[k * 48:(k + 1) * 48].astype(BF16)
+                g2b[half, 2 * q + k // 4, k % 4] = b2[k * 48:(k + 1) * 48].astype(BF16)
+        if h == 0:
+            rs1 = [send(g1b.at[half], rc1, sems, 25, mate), send(g2b.at[half], rc2, sems, 26, mate)]
     vacc[3] = srow
-    rs1 = [send(g1b.at[1 - core], rc1, sems, 25, mate), send(g2b.at[1 - core], rc2, sems, 26, mate)]
 
     def place_d(j, _):
         put_column(df, j + 3, dcv[j])
@@ -329,24 +348,33 @@
     kernel_grads(xf, df, kacc, 2)
 
     def kout(i, _):
-        cur[0, pl.ds(i, 1), :] = jnp.concatenate([jnp.sum(kacc[i, g], axis=0, keepdims=True) for g in range(3)], axis=1)
+        krow[pl.ds(i, 1), :] = jnp.concatenate([jnp.sum(kacc[i, g], axis=0, keepdims=True) for g in range(3)], axis=1)
         return 0
     lax.fori_loop(0, 49, kout, 0)
     rows = [jnp.sum(vacc[i], axis=0, keepdims=True) for i in range(5)]
-    cur[0, 49:56, :] = jnp.zeros((7, C), F32)
-    cur[0, 56:64, :] = jnp.concatenate(rows + [jnp.zeros((3, C), F32)], axis=0)
-
-    def sum_send(stage, at, group):
-        return [send(cur.at[stage], slots.at[at + i], sems, 49 + at + i, dev) for i, dev in enumerate(group)]
-
-    def sum_take(stage, at, copies):
+    krow[49:56, :] = jnp.zeros((7, C), F32)
+    krow[56:64, :] = jnp.concatenate(rows + [jnp.zeros((3, C), F32)], axis=0)
+    cur[...] = krow[...].reshape(2, 2, 16, C)
+
+    def sum_send(stage, groups):
+        copies = []
+        for h, group in enumerate(groups):
+            for i, dev in enumerate(group):
+                k = stage * 6 + h * 3 + i
+                copies.append(send(part_sum.at[stage, h], slots.at[k], sems, 65 + k, dev))
+        return copies
+
+    def sum_take(stage, copies):
         wait_all(copies)
-        total = cur[stage]
-        for i in range(len(copies)):
-            total = total + slots[at + i]
-        cur[stage + 1] = total
-
-    sums = sum_send(0, 0, [mate])
+        for h in range(2):
+            k = stage * 6 + h * 3
+            part_sum[stage + 1, h] = part_sum[stage, h] + slots[k] + slots[k + 1] + slots[k + 2]
+
+    first_sum = send(cur.at[1 - core], mslot, sems, 46, mate)
+    first_sum.wait()
+    for h in range(2):
+        part_sum[0, h] = cur[core, h] + mslot[h]
+    sums = sum_send(0, (ys, zs))
     wait_all(halo_d)
 
     def place_edges(i, _):
@@ -359,9 +387,7 @@
         put_column(df, i, jnp.where(i < 3, left, jnp.where(i < n + 3, own, right)))
         return 0
     lax.fori_loop(0, XC, place_edges, 0)
-    sum_take(0, 0, sums)
-    sums = sum_send(1, 1, ys)
-    back_block(df, tapf, cotb, dimg, 0)
+    back_group(df, tapf, cotb, dimg, 0)
     wait_all(rs2)
 
     def add_second(i, _):
@@ -373,9 +399,9 @@
     for o in range(3):
         rs3.append(send(t1.at[lax.rem(y + o + 1, 4)], ry1.at[o], sems, 33 + o, ys[o]))
         rs3.append(send(t2.at[lax.rem(z + o + 1, 4)], rz2.at[o], sems, 36 + o, zs[o]))
-    sum_take(1, 1, sums)
-    sums = sum_send(2, 4, zs)
-    back_block(df, tapf, cotb, dimg, 1)
+    sum_take(0, sums)
+    sums = sum_send(1, (zs, xs))
+    back_group(df, tapf, cotb, dimg, 1)
     wait_all(rs3)
     u1 = t1[y].astype(F32) + ry1[0].astype(F32) + ry1[1].astype(F32) + ry1[2].astype(F32)
     u2 = t2[z].astype(F32) + rz2[0].astype(F32) + rz2[1].astype(F32) + rz2[2].astype(F32)
@@ -389,9 +415,9 @@
         q = lax.rem(x + o + 1, 4)
         rs4.append(send(p1.at[q], rx1.at[o], sems, 39 + o, xs[o]))
         rs4.append(send(p2.at[q], rx2.at[o], sems, 42 + o, xs[o]))
-    sum_take(2, 4, sums)
-    sums = sum_send(3, 7, xs)
-    back_block(df, tapf, cotb, dimg, 2)
+    sum_take(1, sums)
+    sums = sum_send(2, (xs, ys))
+    back_group(df, tapf, cotb, dimg, 2)
     sr = jnp.where(is_a, offr, 0)
     for i in range(6):
         rsend[i] = dimg[sr + i]
@@ -399,9 +425,27 @@
     wait_all(rs4)
     o1_out[...] = (p1[x] + rx1[0] + rx1[1] + rx1[2]) * SCALE
     o2_out[...] = (p2[x] + rx2[0] + rx2[1] + rx2[2]) * SCALE
-    sum_take(3, 7, sums)
-    small_out[...] = cur[4] * SCALE
+    sum_take(2, sums)
+    total[core] = part_sum[3]
+    last = send(total.at[core], total.at[core], sems, 47, mate)
+    dimg_out[...] = dimg[...]
+    last.wait()
+    small_out[...] = total[...].reshape(64, C) * SCALE
     back.wait()
+    rmate_out[...] = rmate[...]
+
+
+def finish_kernel(widths, place, dimg, rmate, total, o1, o2, out_bias, layer_scale,
+                  d_out, g_kernel, g_bias, g_gain, g_lbias, g_win, g_ibias, g_wout, g_obias, g_scale):
+    me = place[0]
+    core = lax.rem(me, 2)
+    is_a = core == 0
+    wa, wb = widths[me - core], widths[me - core + 1]
+    n0 = (wa + wb + 1) // 2
+    p0 = jnp.where(is_a, 0, n0)
+    mine = jnp.where(is_a, wa, wb)
+    base = jnp.where(is_a, 0, wa)
+    offr = jnp.maximum(n0 - 6, 0)
 
     def place_out(s, _):
         p = base + s
@@ -412,52 +456,79 @@
         d_out[s] = jnp.where(s >= mine, 0.0, val).astype(BF16)
         return 0
     lax.fori_loop(0, CAP, place_out, 0)
-
-
-def fused(widths, feat, cot, s1, s2, taps, vecs):
+    g_kernel[...] = total[0:49]
+
+    def row(i):
+        return total[i:i + 1, :]
+    g_gain[...] = row(56).reshape(C)
+    g_lbias[...] = row(57).reshape(C)
+    g_obias[...] = row(58).reshape(C)
+    g_bias[...] = row(60).reshape(C)
+    ls, ob = layer_scale[...].astype(F32).reshape(1, C), out_bias[...].astype(F32).reshape(1, C)
+    g_scale[...] = ((row(59) + ob * row(58)) / ls).reshape(C)
+    g_win[...] = o1[0:12, 0:C]
+    g_ibias[...] = o1[:, C:512].T[0:1, 0:12].reshape(12)
+    g_wout[...] = o2[0:12]
+
+
+def finish(widths, place, *args):
+    def f(*shape, dtype=F32):
+        return jax.ShapeDtypeStruct(shape, dtype)
+    return pl.pallas_call(
+        finish_kernel,
+        out_shape=(f(CAP, ROWS, C, dtype=BF16), f(49, C), f(C), f(C), f(C), f(12, C), f(12), f(12, C), f(C), f(C)),
+        in_specs=[SMEM] * 2 + [VMEM] * 7,
+        out_specs=[VMEM] * 10,
+        compiler_params=pltpu.CompilerParams(vmem_limit_bytes=24 * 2**20),
+        name="place_results",
+    )(widths, place, *args)
+
+
+def fused(*args):
     def v(*shape, dtype=BF16):
         return pltpu.VMEM(shape, dtype)
     return pl.pallas_call(
         kernel,
         out_shape=(
-            jax.ShapeDtypeStruct((CAP, ROWS, C), BF16),
+            jax.ShapeDtypeStruct((NC, ROWS, C), BF16),
+            jax.ShapeDtypeStruct((6, ROWS, C), BF16),
             jax.ShapeDtypeStruct((64, C), F32),
             jax.ShapeDtypeStruct((16, 512), F32),
             jax.ShapeDtypeStruct((16, C), F32),
         ),
-        in_specs=[SMEM] + [VMEM] * 6,
-        out_specs=[VMEM] * 4,
+        in_specs=[SMEM] + [VMEM] * 10,
+        out_specs=[VMEM] * 5,
         scratch_shapes=[
+            v(16, 512), v(16, C), v(128, 128, dtype=F32),
             v(9, ROWS, C), v(9, ROWS, C), v(3, ROWS, C), v(3, ROWS, C), v(6, ROWS, C), v(6, ROWS, C),
             v(4, 16, 512), v(4, 16, C), v(2, 4, 4, 48, 512), v(2, 4, 4, 48, C),
             v(XC, 3, RP, 128, dtype=F32), v(XC, 3, RP, 128, dtype=F32),
             v(49, 3, 8, 128, dtype=F32), v(49, 3, 8, 128, dtype=F32),
             v(NC, 3, ROWS, 128, dtype=F32), v(NC, ROWS, C),
-            v(512, FF), v(C, FF), v(FF // 256, 256, C), v(512, FF, dtype=F32), v(C, FF, dtype=F32),
+            v(512, FF), v(C, FF), v(FF, C), v(512, FF, dtype=F32), v(C, FF, dtype=F32),
             v(8, 8, C, dtype=F32), v(NC, ROWS, C),
             v(2, 4, 4, 48, 512), v(2, 4, 4, 48, C), v(2, 3, ROWS, C), v(2, 3, ROWS, C),
             v(4, 4, 48, 512), v(4, 4, 48, C), v(4, 4, 48, 512), v(4, 4, 48, C),
             v(3, 4, 48, 512), v(3, 4, 48, C), v(4, 48, 512), v(4, 48, C), v(3, 48, 512), v(3, 48, C),
             v(4, 16, 512, dtype=F32), v(4, 16, C, dtype=F32), v(3, 16, 512, dtype=F32), v(3, 16, C, dtype=F32),
-            v(49, 3, 8, 128, dtype=F32), v(5, 64, C, dtype=F32), v(10, 64, C, dtype=F32),
+            v(49, 3, 8, 128, dtype=F32), v(64, C, dtype=F32), v(2, 2, 16, C, dtype=F32), v(2, 16, C, dtype=F32),
+            v(4, 2, 16, C, dtype=F32), v(18, 16, C, dtype=F32), v(2, 2, 16, C, dtype=F32),
             v(NC, ROWS, C), v(6, ROWS, C), v(6, ROWS, C),
-            pltpu.SemaphoreType.DMA((59,)), pltpu.SemaphoreType.DMA((59,)),
+            pltpu.SemaphoreType.DMA((83,)), pltpu.SemaphoreType.DMA((83,)),
         ],
         compiler_params=pltpu.CompilerParams(collective_id=0, has_side_effects=True, vmem_limit_bytes=60 * 2**20),
         name="block_back",
-    )(widths, feat, cot, s1, s2, taps, vecs)
+    )(*args)
 
 
 def local(features, grad_out, widths, dw_kernel, dw_bias, ln_gain, ln_bias,
           w_in, in_bias, w_out, out_bias, layer_scale):
     feat, cot = jnp.transpose(features, (1, 0, 2)), jnp.transpose(grad_out, (1, 0, 2))
-    s1 = jnp.pad(jnp.concatenate([w_in.T, in_bias[:, None]], axis=1), ((0, 4), (0, 127)))
-    s2 = jnp.pad(w_out, ((0, 4), (0, 0)))
-    vecs = jnp.concatenate([dw_bias, ln_gain, ln_bias, layer_scale]).reshape(4, C).astype(F32)
-    dimg, total, o1, o2 = fused(widths, feat, cot, s1, s2, dw_kernel, vecs)
-    g_scale = (total[59] + out_bias.astype(F32) * total[58]) / layer_scale.astype(F32)
-    return (jnp.transpose(dimg, (1, 0, 2)), total[:49], total[60], total[56], total[57],
-            o1[:12, :C].T, o1[:12, C], o2[:12], total[58], g_scale)
+    place = lax.axis_index("strip").reshape(1)
+    dimg, rmate, total, o1, o2 = fused(widths, feat, cot, w_in.T, in_bias, w_out, dw_kernel,
+                                       dw_bias, ln_gain, ln_bias, layer_scale)
+    outs = finish(widths, place, dimg, rmate, total, o1, o2, out_bias, layer_scale)
+    return (jnp.transpose(outs[0], (1, 0, 2)),) + tuple(outs[1:5]) + (outs[5].T,) + tuple(outs[6:])
 
 
 def solution(mesh):

time: 114 us -> 92.4 us (0.81)
  Pallas kernels: 99 us -> 86.5 us
  local copies, waits for them, and re-layouts: 11.7 us -> 4.73 us
  other arithmetic: 2.66 us -> 0 us
    pallas_call x1 -> x2, Pallas kernels: 99 us -> 86.5 us  [the longest x1 84.2 us: fused(): pl.pallas_call(kernel, out_shape=(jax.ShapeDtypeStruct((NC, ROWS, C), BF1...]
    slice x3 -> x0, local copies, waits for them, and re-layouts: 4.35 us -> none  [the longest x1 1.53 us: local(): total[:49]]
    unnamed x10 -> x16, local copies, waits for them, and re-layouts: 3.31 us -> 4.73 us
    transpose x1 -> x0, local copies, waits for them, and re-layouts: 1.35 us -> none  [local(): o1[:12, :C]]
    concatenate x1 -> x0, other arithmetic: 1.34 us -> none  [local(): jnp.concatenate([w_in.T, in_bias[:, None]], axis=1)]
    pad x1 -> x0, local copies, waits for them, and re-layouts: 1.31 us -> none  [local(): s2 = jnp.pad(w_out, ((0, 4), (0, 0)))]
where the time goes in v3:
time: 92.4 us; the launch traced here: 92 us
  Pallas kernels  86.5 us (94%)
  local copies, waits for them, and re-layouts  4.73 us (5%)
    pallas_call x1, Pallas kernels, fused(): pl.pallas_call(kernel, out_shape=(jax.ShapeDtypeStruct((NC, ROWS, C), BF1...  84.2 us
    unnamed x16, local copies, waits for them, and re-layouts  4.73 us
    pallas_call x1, Pallas kernels, finish(): pl.pallas_call(finish_kernel, out_shape=(f(CAP, ROWS, C, dtype=BF16), f(4...  2.34 us

profile of v3, /device:TPU:1, one launch (start us, length us, event | category | flops | bytes accessed | tf_op | source)
XLA Modules:
  0.0 92.0 jit_solution(12405290962474767731)
XLA Ops:
  0.7 0.0 copy-start.5
  0.7 0.0 copy-start.6
  0.7 0.0 copy-start.7
  0.7 84.2 %block_back.1 = (bf16[12,128,384]{2,1,0:T(8,128)(2,1)}, bf16[6,128,384]{2,1,0:T(8,128)(2,1)}, f32[64,384]{1,0:T(8,128)}, f32[16,512]{1,0:T(8,128)}, f32[16,384]{1,0:T(8,128)}) custom-call(s32[128]{0:T(128)} %widths.3, bf16[15,128,384]{2,1,0:T(8,128)(2,1)} %bitcast.6, bf16[15,128,384]{2,1,0:T(8,128)(2,1)} %bitcast.7, bf16[12,384]{1,0:T(8,128)(2,1)} %bitcast.8, ...), custom_call_target="tpu_custom_call" | custom-call | tf_op jit(solution)/shard_map/block_back/pallas_call | solution.py:490
  84.9 0.0 copy-done.5
  84.9 0.0 copy-done.6
  84.9 0.0 copy-done.7
  84.9 0.0 copy-start
  84.9 1.3 %copy-done = bf16[12,128,384]{2,1,0:T(8,128)(2,1)S(1)} copy-done((bf16[12,128,384]{2,1,0:T(8,128)(2,1)S(1)}, bf16[12,128,384]{2,1,0:T(8,128)(2,1)}, u32[]{:S(2)}) %copy-start) | copy-done | bytes 1179672
  86.2 0.0 copy-start.1
  86.2 1.1 %copy-done.1 = bf16[6,128,384]{2,1,0:T(8,128)(2,1)S(1)} copy-done((bf16[6,128,384]{2,1,0:T(8,128)(2,1)S(1)}, bf16[6,128,384]{2,1,0:T(8,128)(2,1)}, u32[]{:S(2)}) %copy-start.1) | copy-done | bytes 589848
  87.3 0.0 copy-start.2
  87.3 0.9 copy-done.2
  88.1 0.0 copy-start.3
  88.1 0.8 copy-done.3
  88.9 0.0 copy-start.4
  88.9 0.7 copy-done.4
  89.6 2.3 %place_results.1 = (bf16[15,128,384]{2,1,0:T(8,128)(2,1)}, f32[49,384]{1,0:T(8,128)}, f32[384]{0:T(512)}, f32[384]{0:T(512)}, f32[384]{0:T(512)}, /*index=5*/f32...) custom-call(s32[128]{0:T(128)S(1)} %copy-done.6, s32[1]{0:T(128)} %bitcast.place, ...), custom_call_target="tpu_custom_call" | custom-call | tf_op jit(solution)/shard_map/place_results/pallas_call | solution.py:477
Async XLA Ops:
  0.7 84.2 %copy-start.5 = (bf16[384]{0:T(512)(128)(2,1)S(1)}, bf16[384]{0:T(512)(128)(2,1)}, u32[]{:S(2)}) copy-start(bf16[384]{0:T(512)(128)(2,1)} %layer_scale.3) | copy-start | bytes 2308
  0.7 84.2 %copy-start.6 = (s32[128]{0:T(128)S(1)}, s32[128]{0:T(128)}, u32[]{:S(2)}) copy-start(s32[128]{0:T(128)} %widths.3) | copy-start | bytes 1540
  0.7 84.2 %copy-start.7 = (bf16[384]{0:T(512)(128)(2,1)S(1)}, bf16[384]{0:T(512)(128)(2,1)}, u32[]{:S(2)}) copy-start(bf16[384]{0:T(512)(128)(2,1)} %out_bias.1) | copy-start | bytes 2308
  84.9 1.3 %copy-start = (bf16[12,128,384]{2,1,0:T(8,128)(2,1)S(1)}, bf16[12,128,384]{2,1,0:T(8,128)(2,1)}, u32[]{:S(2)}) copy-start(bf16[12,128,384]{2,1,0:T(8,128)(2,1)} %get-tuple-element.25.dimg) | copy-start | bytes 3538948
  86.2 1.1 %copy-start.1 = (bf16[6,128,384]{2,1,0:T(8,128)(2,1)S(1)}, bf16[6,128,384]{2,1,0:T(8,128)(2,1)}, u32[]{:S(2)}) copy-start(bf16[6,128,384]{2,1,0:T(8,128)(2,1)} %get-tuple-element.26.rmate) | copy-start | bytes 1769476
  87.3 0.9 copy-start.2
  88.1 0.8 copy-start.3
  88.9 0.7 copy-start.4

commit v4 on v3

--- a/solution.py
+++ b/solution.py
@@ -14,6 +14,7 @@
 XC = NC + 6
 RP = ROWS + 16
 T = 2 * ROWS
+TOK = NC * ROWS
 F32, BF16 = jnp.float32, jnp.bfloat16
 VMEM = pl.BlockSpec(memory_space=pltpu.VMEM)
 SMEM = pl.BlockSpec(memory_space=pltpu.SMEM)
@@ -117,8 +118,9 @@
     return x.reshape(T // 8, 8, C).sum(0)
 
 
-def mlp_step(s, conv, cotb, vecs, w1, w2, w1t, g1, g2, vacc, dcv):
+def norm_step(s, conv, cotb, vecs, nrm, nrm_t, dm, dm_t, nraw_s, inv_s, vacc):
     bias, gain, lbias, ls = vecs
+    at = pl.ds(pl.multiple_of(s * T, T), T)
     one_col = (lax.broadcasted_iota(jnp.int32, (T, 128), 1) == 0).astype(BF16)
     v = jnp.concatenate([conv[pl.ds(2 * s, 2), g].reshape(T, 128) for g in range(3)], axis=1) + bias
     v = v.astype(BF16).astype(F32)
@@ -129,26 +131,36 @@
     normed = jnp.concatenate([(nraw * gain + lbias).astype(BF16), one_col], axis=1)
     dmlp = (cotb[pl.ds(2 * s, 2)].reshape(T, C).astype(F32) * ls).astype(BF16)
     vacc[2] += part(dmlp.astype(F32))
-    normed_t = normed.T
-    dmlp_t = dmlp.T
-    blocks = [slice(f * 256, f * 256 + 256) for f in range(FF // 256)]
-
-    def front(sl):
-        return (jnp.dot(normed, w1[:, sl], preferred_element_type=F32),
-                jnp.dot(dmlp, w2[:, sl], preferred_element_type=F32))
-    acts, dpres = [], []
-    ahead = front(blocks[0])
-    for f in range(len(blocks)):
+    nrm[at, :] = normed
+    nrm_t[:, at] = normed.T
+    dm[at, :] = dmlp
+    dm_t[:, at] = dmlp.T
+    nraw_s[at, :] = nraw
+    inv_s[at, :] = jnp.broadcast_to(inv, (T, 128))
+
+
+def hidden_block(first, nrm, dm, wa, wb, wrows, act_s, dpre_s, dn_s):
+    ats = [slice(k * T, k * T + T) for k in range(TOK // T)]
+
+    def front(at):
+        return (jnp.dot(nrm[at, :], wa[...], preferred_element_type=F32),
+                jnp.dot(dm[at, :], wb[...], preferred_element_type=F32))
+    ahead = front(ats[0])
+    for i, at in enumerate(ats):
         pre, dact = ahead
-        if f + 1 < len(blocks):
-            ahead = front(blocks[f + 1])
+        if i + 1 < len(ats):
+            ahead = front(ats[i + 1])
         act, slope = gelu_parts(pre)
-        acts.append(act.astype(BF16))
-        dpres.append((dact * slope).astype(BF16))
-    dn = jnp.dot(jnp.concatenate(dpres, axis=1), w1t[...], preferred_element_type=F32)
-    for sl, act, dpre in zip(blocks, acts, dpres):
-        g1[:, sl] += jnp.dot(normed_t, dpre, preferred_element_type=F32)
-        g2[:, sl] += jnp.dot(dmlp_t, act, preferred_element_type=F32)
+        act_s[at, :] = act.astype(BF16)
+        dpre = (dact * slope).astype(BF16)
+        dpre_s[at, :] = dpre
+        dn = jnp.dot(dpre, wrows[...], preferred_element_type=F32)
+        dn_s[at, :] = dn if first else dn_s[at, :] + dn
+
+
+def denorm_step(s, dn_s, nraw_s, inv_s, gain, vacc, dcv):
+    at = pl.ds(pl.multiple_of(s * T, T), T)
+    dn, nraw, inv = dn_s[at, :], nraw_s[at, :], inv_s[at, 0:1]
     vacc[0] += part(dn * nraw)
     vacc[1] += part(dn)
     sc = dn * gain
@@ -176,13 +188,14 @@
         copy.wait()
 
 
-def kernel(widths, feat, cot, w_in_t, in_bias, w_out, taps, dw_bias, ln_gain, ln_bias, layer_scale,
+def kernel(widths, feat_any, cot_any, w_in_t, in_bias, w_out, taps, dw_bias, ln_gain, ln_bias, layer_scale,
            dimg_out, rmate_out, small_out, o1_out, o2_out,
-           s1, s2, sbias,
+           feat, cot, s1, s2, sbias,
            xsend, xmate, hsend, xhalo, csend, cmate,
-           bx1, bx2, w1g, w2g, xf, df, tapb, tapf, conv, cotb, w1, w2, w1c, g1, g2, vacc, dcv,
+           bx1, bx2, w1g, w2g, xf, df, tapb, tapf, conv, cotb, nrm, nrm_t, dm, dm_t, nraw_s, inv_s, dn_s,
+           act_a, dpre_a, act_b, dpre_b, mwa, mwb, wr, vacc, dcv,
            g1b, g2b, dsend, dhalo, rc1, rc2, c1, c2, rz1, ry2, t1, t2, ry1, rz2, p1, p2, rx1, rx2,
-           kacc, krow, cur, mslot, part_sum, slots, total, dimg, rsend, rmate, ssem, rsem):
+           kacc, krow, cur, mslot, part_sum, slots, total, dimg, rsend, rmate, ssem, rsem, lsem):
     me = lax.axis_index("strip")
     core = lax.rem(me, 2)
     y = lax.rem(me // 2, 4)
@@ -208,14 +221,11 @@
     for dev in xs + ys + zs + [mate, outer]:
         pl.semaphore_signal(barrier, inc=1, device_id=(dev,), device_id_type=MESH)
 
+    loads = [pltpu.make_async_copy(feat_any, feat, lsem.at[0]), pltpu.make_async_copy(cot_any, cot, lsem.at[1])]
+    for load in loads:
+        load.start()
     s9, s6 = jnp.where(is_a, off9, 0), jnp.where(is_a, off6, 0)
-    for i in range(9):
-        xsend[i] = feat[s9 + i]
-    for i in range(6):
-        csend[i] = cot[s6 + i]
     h3 = jnp.where(is_a, 0, jnp.maximum(wb - 3, 0))
-    for i in range(3):
-        hsend[i] = feat[h3 + i]
     sbias[...] = jnp.zeros_like(sbias)
     sbias[0:1, 0:12] = in_bias[...].astype(F32).reshape(1, 12)
     s1[:, C:512] = sbias[...].T[0:16].astype(BF16)
@@ -224,24 +234,48 @@
     s2[...] = jnp.concatenate([w_out[...].astype(F32), pad4], axis=0).astype(BF16)
     pl.semaphore_wait(barrier, 11)
 
-    halo_in = [send(hsend, xhalo, sems, 0, outer), send(xsend, xmate, sems, 1, mate)]
     first = []
     for o in range(3):
         first.append(send(s1, bx1.at[x], sems, 2 + o, xs[o]))
         first.append(send(s2, bx2.at[x], sems, 5 + o, xs[o]))
-    cot_in = send(csend, cmate, sems, 8, mate)
     bx1[x] = s1[...]
     bx2[x] = s2[...]
+    loads[0].wait()
+    for i in range(3):
+        hsend[i] = feat[h3 + i]
+    halo_in = [send(hsend, xhalo, sems, 0, outer)]
+    for i in range(9):
+        xsend[i] = feat[s9 + i]
+    halo_in.append(send(xsend, xmate, sems, 1, mate))
+    wait_all(first)
+    for ch in range(3):
+        rows4 = slice(ch * 4, ch * 4 + 4)
+        w1g[core, ch, z, y] = jnp.concatenate([bx1[q].astype(F32)[rows4] for q in range(4)], axis=0).astype(BF16)
+        w2g[core, ch, z, y] = jnp.concatenate([bx2[q].astype(F32)[rows4] for q in range(4)], axis=0).astype(BF16)
+    second = []
+    for o in range(3):
+        second.append(send(w1g.at[core, :, z, y], w1g.at[core, :, z, y], sems, 9 + o, ys[o]))
+        second.append(send(w2g.at[core, :, z, y], w2g.at[core, :, z, y], sems, 12 + o, zs[o]))
+    loads[1].wait()
+    for i in range(6):
+        csend[i] = cot[s6 + i]
+    cot_in = send(csend, cmate, sems, 8, mate)
     fill_taps(taps, tapb, False)
     clear_pads(xf)
     clear_pads(df)
-    wait_all(first)
-    w1g[core, z, y] = jnp.concatenate([bx1[q].astype(F32)[:12] for q in range(4)], axis=0).astype(BF16)
-    w2g[core, z, y] = jnp.concatenate([bx2[q].astype(F32)[:12] for q in range(4)], axis=0).astype(BF16)
-    second = []
-    for o in range(3):
-        second.append(send(w1g.at[core, z, y], w1g.at[core, z, y], sems, 9 + o, ys[o]))
-        second.append(send(w2g.at[core, z, y], w2g.at[core, z, y], sems, 12 + o, zs[o]))
+    wait_all(second)
+    third = []
+    for ch in range(3):
+        copies = []
+        for o in range(3):
+            copies.append(send(w1g.at[core, ch, z], w1g.at[core, ch, z], sems, 83 + ch * 6 + o, zs[o]))
+            copies.append(send(w2g.at[core, ch, :, y], w2g.at[core, ch, :, y], sems, 83 + ch * 6 + 3 + o, ys[o]))
+        third.append(copies)
+
+    def pass_on(ch):
+        wait_all(third[ch])
+        return [send(w1g.at[core, ch], w1g.at[core, ch], sems, 101 + 2 * ch, mate),
+                send(w2g.at[core, ch], w2g.at[core, ch], sems, 102 + 2 * ch, mate)]
     wait_all(halo_in)
 
     def place_x(i, _):
@@ -257,13 +291,6 @@
         put_column(xf, i, jnp.where(gone, 0.0, val))
         return 0
     lax.fori_loop(0, XC, place_x, 0)
-    wait_all(second)
-    third1, third2 = [], []
-    for o in range(3):
-        third1.append(send(w1g.at[core, z], w1g.at[core, z], sems, 15 + o, zs[o]))
-        third2.append(send(w2g.at[core, :, y], w2g.at[core, :, y], sems, 18 + o, ys[o]))
-    fourth = [send(w1g.at[core, z], w1g.at[core, z], sems, 21, mate),
-              send(w2g.at[core, :, y], w2g.at[core, :, y], sems, 22, mate)]
     conv_group(xf, tapb, conv, 0)
     cot_in.wait()
 
@@ -277,32 +304,72 @@
         return 0
     lax.fori_loop(0, NC, place_cot, 0)
     conv_group(xf, tapb, conv, 1)
-    for o in range(3):
-        zb, yb = lax.rem(z + 3 - o, 4), lax.rem(y + 3 - o, 4)
-        third1[o].wait()
-        fourth.append(send(w1g.at[core, zb], w1g.at[core, zb], sems, 59 + o, mate))
-        third2[o].wait()
-        fourth.append(send(w2g.at[core, :, yb], w2g.at[core, :, yb], sems, 62 + o, mate))
+    passed = [pass_on(0)]
     conv_group(xf, tapb, conv, 2)
     conv[NC - 1] = jnp.zeros((3, ROWS, 128), F32)
-    fill_taps(taps, tapf, True)
     vacc[...] = jnp.zeros_like(vacc)
-    g1[...] = jnp.zeros_like(g1)
-    g2[...] = jnp.zeros_like(g2)
-    wait_all(fourth)
-    w1full = w1g[...].reshape(FF, 512)
-    w2full = w2g[...].reshape(FF, C)
-    for f in range(FF // 256):
-        sl = slice(f * 256, f * 256 + 256)
-        w1[:, sl] = w1full[sl].T
-        w2[:, sl] = w2full[sl].T
-        w1c[sl, :] = w1full[sl, :C]
     vecs = tuple(ref[...].astype(F32).reshape(1, C) for ref in (dw_bias, ln_gain, ln_bias, layer_scale))
 
-    def step(s, _):
-        mlp_step(s, conv, cotb, vecs, w1, w2, w1c, g1, g2, vacc, dcv)
-        return 0
-    lax.fori_loop(0, NC // 2, step, 0)
+    def before(s, _):
+        norm_step(s, conv, cotb, vecs, nrm, nrm_t, dm, dm_t, nraw_s, inv_s, vacc)
+        return 0
+    lax.fori_loop(0, NC // 2, before, 0)
+
+    sums_w = [jnp.zeros((8, C), F32)]
+    rs1, rs2 = {}, []
+
+    def weight_grads(ch, own_half, act_s, dpre_s):
+        half = core if own_half else 1 - core
+        b1 = jnp.dot(nrm_t[...], dpre_s[...], preferred_element_type=F32).T
+        b2 = jnp.dot(dm_t[...], act_s[...], preferred_element_type=F32).T
+        sums_w[0] += (b2 * w2g[half, ch].reshape(256, C).astype(F32)).reshape(32, 8, C).sum(0)
+        to1, to2 = (c1, c2) if own_half else (g1b, g2b)
+        to1[ch] = b1.astype(BF16).reshape(4, 4, 16, 512)
+        to2[ch] = b2.astype(BF16).reshape(4, 4, 16, C)
+
+    def give(ch):
+        rs1[ch] = [send(g1b.at[ch], rc1.at[ch], sems, 125 + 2 * ch, mate),
+                   send(g2b.at[ch], rc2.at[ch], sems, 126 + 2 * ch, mate)]
+
+    def join(ch):
+        wait_all(rs1[ch])
+        for q in range(4):
+            c1[ch, q] = (c1[ch, q].astype(F32) + rc1[ch, q].astype(F32)).astype(BF16)
+            c2[ch, q] = (c2[ch, q].astype(F32) + rc2[ch, q].astype(F32)).astype(BF16)
+        copies = []
+        for o in range(3):
+            k = 107 + ch * 6 + o
+            copies.append(send(c1.at[ch, lax.rem(z + o + 1, 4)], rz1.at[ch, o], sems, k, zs[o]))
+            copies.append(send(c2.at[ch, :, lax.rem(y + o + 1, 4)], ry2.at[ch, o], sems, k + 3, ys[o]))
+        rs2.append(copies)
+
+    order = [(0, True), (0, False), (1, False), (1, True), (2, False), (2, True)]
+    hold = ((act_a, dpre_a), (act_b, dpre_b))
+    for turn, (ch, own_half) in enumerate(order):
+        half = core if own_half else 1 - core
+        if turn in (1, 2):
+            passed.append(pass_on(turn))
+        if not own_half:
+            wait_all(passed[ch])
+        mwa[...] = w1g[half, ch].reshape(256, 512).T
+        mwb[...] = w2g[half, ch].reshape(256, C).T
+        wr[...] = w1g[half, ch].reshape(256, 512)[:, 0:C]
+        if turn > 0:
+            weight_grads(*order[turn - 1], *hold[(turn - 1) % 2])
+        hidden_block(turn == 0, nrm, dm, mwa, mwb, wr, *hold[turn % 2], dn_s)
+        if turn > 0 and not order[turn - 1][1]:
+            give(order[turn - 1][0])
+        if turn in (3, 4):
+            join(turn - 3)
+    weight_grads(*order[5], *hold[1])
+    join(2)
+    srow = sums_w[0]
+    vacc[3] = srow
+
+    def after(s, _):
+        denorm_step(s, dn_s, nraw_s, inv_s, vecs[1], vacc, dcv)
+        return 0
+    lax.fori_loop(0, NC // 2, after, 0)
 
     last_at = jnp.maximum(n - 3, 0)
     inner_at, outer_at = jnp.where(is_a, last_at, 0), jnp.where(is_a, 0, last_at)
@@ -310,41 +377,28 @@
         dsend[0, i] = dcv[inner_at + i]
         dsend[1, i] = dcv[outer_at + i]
     halo_d = [send(dsend.at[0], dhalo.at[0], sems, 23, mate), send(dsend.at[1], dhalo.at[1], sems, 24, outer)]
-    srow = jnp.zeros((8, C), F32)
-    rs1 = []
-    for h in range(2):
-        half = 1 - core if h == 0 else core
-        for q in range(2):
-            at = pl.ds(pl.multiple_of(half * 768 + q * 384, 128), 384)
-            b1 = g1[:, at].T
-            b2 = g2[:, at].T
-            wrow = w2g[half, pl.ds(2 * q, 2)].reshape(384, C)
-            srow += (b2 * wrow.astype(F32)).reshape(48, 8, C).sum(0)
-            for k in range(8):
-                g1b[half, 2 * q + k // 4, k % 4] = b1[k * 48:(k + 1) * 48].astype(BF16)
-                g2b[half, 2 * q + k // 4, k % 4] = b2[k * 48:(k + 1) * 48].astype(BF16)
-        if h == 0:
-            rs1 = [send(g1b.at[half], rc1, sems, 25, mate), send(g2b.at[half], rc2, sems, 26, mate)]
-    vacc[3] = srow
-
     def place_d(j, _):
         put_column(df, j + 3, dcv[j])
         return 0
     lax.fori_loop(0, NC, place_d, 0)
     kernel_grads(xf, df, kacc, 0)
-    wait_all(rs1)
-
-    def add_first(i, _):
-        zi, yi = i // 4, lax.rem(i, 4)
-        c1[zi, yi] = (g1b[core, zi, yi].astype(F32) + rc1[zi, yi].astype(F32)).astype(BF16)
-        c2[zi, yi] = (g2b[core, zi, yi].astype(F32) + rc2[zi, yi].astype(F32)).astype(BF16)
-        return 0
-    lax.fori_loop(0, 16, add_first, 0)
-    rs2 = []
+    fill_taps(taps, tapf, True)
+    kernel_grads(xf, df, kacc, 1)
+    for copies in rs2:
+        wait_all(copies)
+    rs3 = []
+
+    def add_second(i, _):
+        ch, q = i // 4, lax.rem(i, 4)
+        t1[ch, q] = (c1[ch, z, q].astype(F32) + rz1[ch, 0, q].astype(F32) + rz1[ch, 1, q].astype(F32)
+                     + rz1[ch, 2, q].astype(F32)).astype(BF16)
+        t2[ch, q] = (c2[ch, q, y].astype(F32) + ry2[ch, 0, q].astype(F32) + ry2[ch, 1, q].astype(F32)
+                     + ry2[ch, 2, q].astype(F32)).astype(BF16)
+        return 0
+    lax.fori_loop(0, 12, add_second, 0)
     for o in range(3):
-        rs2.append(send(c1.at[lax.rem(z + o + 1, 4)], rz1.at[o], sems, 27 + o, zs[o]))
-        rs2.append(send(c2.at[:, lax.rem(y + o + 1, 4)], ry2.at[o], sems, 30 + o, ys[o]))
-    kernel_grads(xf, df, kacc, 1)
+        rs3.append(send(t1.at[:, lax.rem(y + o + 1, 4)], ry1.at[o], sems, 33 + o, ys[o]))
+        rs3.append(send(t2.at[:, lax.rem(z + o + 1, 4)], rz2.at[o], sems, 36 + o, zs[o]))
     kernel_grads(xf, df, kacc, 2)
 
     def kout(i, _):
@@ -375,6 +429,21 @@
     for h in range(2):
         part_sum[0, h] = cur[core, h] + mslot[h]
     sums = sum_send(0, (ys, zs))
+    wait_all(rs3)
+    for ch in range(3):
+        u1 = (t1[ch, y].astype(F32) + ry1[0, ch].astype(F32)) + (ry1[1, ch].astype(F32) + ry1[2, ch].astype(F32))
+        u2 = (t2[ch, z].astype(F32) + rz2[0, ch].astype(F32)) + (rz2[1, ch].astype(F32) + rz2[2, ch].astype(F32))
+        for q in range(4):
+            p1[q, ch * 4:ch * 4 + 4, :] = u1[q * 4:q * 4 + 4]
+            p2[q, ch * 4:ch * 4 + 4, :] = u2[q * 4:q * 4 + 4]
+    for q in range(4):
+        p1[q, 12:16, :] = jnp.zeros((4, 512), F32)
+        p2[q, 12:16, :] = jnp.zeros((4, C), F32)
+    rs4 = []
+    for o in range(3):
+        q = lax.rem(x + o + 1, 4)
+        rs4.append(send(p1.at[q], rx1.at[o], sems, 39 + o, xs[o]))
+        rs4.append(send(p2.at[q], rx2.at[o], sems, 42 + o, xs[o]))
     wait_all(halo_d)
 
     def place_edges(i, _):
@@ -388,33 +457,9 @@
         return 0
     lax.fori_loop(0, XC, place_edges, 0)
     back_group(df, tapf, cotb, dimg, 0)
-    wait_all(rs2)
-
-    def add_second(i, _):
-        t1[i] = (c1[z, i].astype(F32) + rz1[0, i].astype(F32) + rz1[1, i].astype(F32) + rz1[2, i].astype(F32)).astype(BF16)
-        t2[i] = (c2[i, y].astype(F32) + ry2[0, i].astype(F32) + ry2[1, i].astype(F32) + ry2[2, i].astype(F32)).astype(BF16)
-        return 0
-    lax.fori_loop(0, 4, add_second, 0)
-    rs3 = []
-    for o in range(3):
-        rs3.append(send(t1.at[lax.rem(y + o + 1, 4)], ry1.at[o], sems, 33 + o, ys[o]))
-        rs3.append(send(t2.at[lax.rem(z + o + 1, 4)], rz2.at[o], sems, 36 + o, zs[o]))
     sum_take(0, sums)
     sums = sum_send(1, (zs, xs))
     back_group(df, tapf, cotb, dimg, 1)
-    wait_all(rs3)
-    u1 = t1[y].astype(F32) + ry1[0].astype(F32) + ry1[1].astype(F32) + ry1[2].astype(F32)
-    u2 = t2[z].astype(F32) + rz2[0].astype(F32) + rz2[1].astype(F32) + rz2[2].astype(F32)
-    for q in range(4):
-        p1[q, 0:12, :] = u1[q * 12:q * 12 + 12]
-        p2[q, 0:12, :] = u2[q * 12:q * 12 + 12]
-        p1[q, 12:16, :] = jnp.zeros((4, 512), F32)
-        p2[q, 12:16, :] = jnp.zeros((4, C), F32)
-    rs4 = []
-    for o in range(3):
-        q = lax.rem(x + o + 1, 4)
-        rs4.append(send(p1.at[q], rx1.at[o], sems, 39 + o, xs[o]))
-        rs4.append(send(p2.at[q], rx2.at[o], sems, 42 + o, xs[o]))
     sum_take(1, sums)
     sums = sum_send(2, (xs, ys))
     back_group(df, tapf, cotb, dimg, 2)
@@ -479,7 +524,7 @@
         out_shape=(f(CAP, ROWS, C, dtype=BF16), f(49, C), f(C), f(C), f(C), f(12, C), f(12), f(12, C), f(C), f(C)),
         in_specs=[SMEM] * 2 + [VMEM] * 7,
         out_specs=[VMEM] * 10,
-        compiler_params=pltpu.CompilerParams(vmem_limit_bytes=24 * 2**20),
+        compiler_params=pltpu.CompilerParams(vmem_limit_bytes=60 * 2**20),
         name="place_results",
     )(widths, place, *args)
 
@@ -496,25 +541,26 @@
             jax.ShapeDtypeStruct((16, 512), F32),
             jax.ShapeDtypeStruct((16, C), F32),
         ),
-        in_specs=[SMEM] + [VMEM] * 10,
+        in_specs=[SMEM] + [pl.BlockSpec(memory_space=pl.ANY)] * 2 + [VMEM] * 8,
         out_specs=[VMEM] * 5,
         scratch_shapes=[
-            v(16, 512), v(16, C), v(128, 128, dtype=F32),
+            v(CAP, ROWS, C), v(CAP, ROWS, C), v(16, 512), v(16, C), v(128, 128, dtype=F32),
             v(9, ROWS, C), v(9, ROWS, C), v(3, ROWS, C), v(3, ROWS, C), v(6, ROWS, C), v(6, ROWS, C),
-            v(4, 16, 512), v(4, 16, C), v(2, 4, 4, 48, 512), v(2, 4, 4, 48, C),
+            v(4, 16, 512), v(4, 16, C), v(2, 3, 4, 4, 16, 512), v(2, 3, 4, 4, 16, C),
             v(XC, 3, RP, 128, dtype=F32), v(XC, 3, RP, 128, dtype=F32),
             v(49, 3, 8, 128, dtype=F32), v(49, 3, 8, 128, dtype=F32),
             v(NC, 3, ROWS, 128, dtype=F32), v(NC, ROWS, C),
-            v(512, FF), v(C, FF), v(FF, C), v(512, FF, dtype=F32), v(C, FF, dtype=F32),
+            v(TOK, 512), v(512, TOK), v(TOK, C), v(C, TOK), v(TOK, C, dtype=F32), v(TOK, 128, dtype=F32), v(TOK, C, dtype=F32),
+            v(TOK, 256), v(TOK, 256), v(TOK, 256), v(TOK, 256), v(512, 256), v(C, 256), v(256, C),
             v(8, 8, C, dtype=F32), v(NC, ROWS, C),
-            v(2, 4, 4, 48, 512), v(2, 4, 4, 48, C), v(2, 3, ROWS, C), v(2, 3, ROWS, C),
-            v(4, 4, 48, 512), v(4, 4, 48, C), v(4, 4, 48, 512), v(4, 4, 48, C),
-            v(3, 4, 48, 512), v(3, 4, 48, C), v(4, 48, 512), v(4, 48, C), v(3, 48, 512), v(3, 48, C),
+            v(3, 4, 4, 16, 512), v(3, 4, 4, 16, C), v(2, 3, ROWS, C), v(2, 3, ROWS, C),
+            v(3, 4, 4, 16, 512), v(3, 4, 4, 16, C), v(3, 4, 4, 16, 512), v(3, 4, 4, 16, C),
+            v(3, 3, 4, 16, 512), v(3, 3, 4, 16, C), v(3, 4, 16, 512), v(3, 4, 16, C), v(3, 3, 16, 512), v(3, 3, 16, C),
             v(4, 16, 512, dtype=F32), v(4, 16, C, dtype=F32), v(3, 16, 512, dtype=F32), v(3, 16, C, dtype=F32),
             v(49, 3, 8, 128, dtype=F32), v(64, C, dtype=F32), v(2, 2, 16, C, dtype=F32), v(2, 16, C, dtype=F32),
             v(4, 2, 16, C, dtype=F32), v(18, 16, C, dtype=F32), v(2, 2, 16, C, dtype=F32),
             v(NC, ROWS, C), v(6, ROWS, C), v(6, ROWS, C),
-            pltpu.SemaphoreType.DMA((83,)), pltpu.SemaphoreType.DMA((83,)),
+            pltpu.SemaphoreType.DMA((131,)), pltpu.SemaphoreType.DMA((131,)), pltpu.SemaphoreType.DMA((2,)),
         ],
         compiler_params=pltpu.CompilerParams(collective_id=0, has_side_effects=True, vmem_limit_bytes=60 * 2**20),
         name="block_back",

time: 92.4 us -> 84.3 us (0.912)
  local copies, waits for them, and re-layouts: 4.73 us -> 0 us
  Pallas kernels: 86.5 us -> 83.3 us
    unnamed x16 -> x0, local copies, waits for them, and re-layouts: 4.73 us -> none
    pallas_call x1, Pallas kernels: 84.2 us -> 80 us  [fused(): pl.pallas_call(kernel, out_shape=(jax.ShapeDtypeStruct((NC, ROWS, C), BF1...]
    pallas_call x1, Pallas kernels: 2.34 us -> 3.3 us  [finish(): pl.pallas_call(finish_kernel, out_shape=(f(CAP, ROWS, C, dtype=BF16), f(4...]
where the time goes in v4:
time: 84.3 us; the launch traced here: 84.1 us
  Pallas kernels  83.3 us (99%)
    pallas_call x1, Pallas kernels, fused(): pl.pallas_call(kernel, out_shape=(jax.ShapeDtypeStruct((NC, ROWS, C), BF1...  80 us
    pallas_call x1, Pallas kernels, finish(): pl.pallas_call(finish_kernel, out_shape=(f(CAP, ROWS, C, dtype=BF16), f(4...  3.3 us

profile of v4, /device:TPU:1, one launch (start us, length us, event | category | flops | bytes accessed | tf_op | source)
XLA Modules:
  0.0 84.1 jit_solution(18415950005734212872)
XLA Ops:
  0.6 80.0 %block_back.1 = (bf16[12,128,384]{2,1,0:T(8,128)(2,1)}, bf16[6,128,384]{2,1,0:T(8,128)(2,1)}, f32[64,384]{1,0:T(8,128)}, f32[16,512]{1,0:T(8,128)}, f32[16,384]{1,0:T(8,128)}) custom-call(s32[128]{0:T(128)} %widths.3, bf16[15,128,384]{2,1,0:T(8,128)(2,1)} %bitcast.6, bf16[15,128,384]{2,1,0:T(8,128)(2,1)} %bitcast.7, bf16[12,384]{1,0:T(8,128)(2,1)} %bitcast.8, ...), custom_call_target="tpu_custom_call" | custom-call | tf_op jit(solution)/shard_map/block_back/pallas_call | solution.py:535
  80.7 3.3 %place_results.1 = (bf16[15,128,384]{2,1,0:T(8,128)(2,1)}, f32[49,384]{1,0:T(8,128)}, f32[384]{0:T(512)}, f32[384]{0:T(512)}, f32[384]{0:T(512)}, /*index=5*/f32...) custom-call(s32[128]{0:T(128)} %widths.3, s32[1]{0:T(128)} %bitcast.place, ...), custom_call_target="tpu_custom_call" | custom-call | tf_op jit(solution)/shard_map/place_results/pallas_call | solution.py:522

commit v5 on v4

--- a/solution.py
+++ b/solution.py
@@ -191,7 +191,7 @@
 def kernel(widths, feat_any, cot_any, w_in_t, in_bias, w_out, taps, dw_bias, ln_gain, ln_bias, layer_scale,
            dimg_out, rmate_out, small_out, o1_out, o2_out,
            feat, cot, s1, s2, sbias,
-           xsend, xmate, hsend, xhalo, csend, cmate,
+           xsend, xmate, hsend, xhalo_a, xhalo_b, xhalo_c, csend, cmate,
            bx1, bx2, w1g, w2g, xf, df, tapb, tapf, conv, cotb, nrm, nrm_t, dm, dm_t, nraw_s, inv_s, dn_s,
            act_a, dpre_a, act_b, dpre_b, mwa, mwb, wr, vacc, dcv,
            g1b, g2b, dsend, dhalo, rc1, rc2, c1, c2, rz1, ry2, t1, t2, ry1, rz2, p1, p2, rx1, rx2,
@@ -243,10 +243,18 @@
     loads[0].wait()
     for i in range(3):
         hsend[i] = feat[h3 + i]
-    halo_in = [send(hsend, xhalo, sems, 0, outer)]
+    xhalo = (xhalo_a, xhalo_b, xhalo_c)
+    halo_in = []
+    for g in range(3):
+        lanes = pl.ds(g * 128, 128)
+        halo_in.append(send(hsend.at[:, :, lanes], xhalo[g], sems, (0, 59, 60)[g], outer))
     for i in range(9):
         xsend[i] = feat[s9 + i]
-    halo_in.append(send(xsend, xmate, sems, 1, mate))
+    mate_in = send(xsend, xmate, sems, 1, mate)
+    fill_taps(taps, tapb, False)
+    fill_taps(taps, tapf, True)
+    clear_pads(xf)
+    clear_pads(df)
     wait_all(first)
     for ch in range(3):
         rows4 = slice(ch * 4, ch * 4 + 4)
@@ -256,13 +264,31 @@
     for o in range(3):
         second.append(send(w1g.at[core, :, z, y], w1g.at[core, :, z, y], sems, 9 + o, ys[o]))
         second.append(send(w2g.at[core, :, z, y], w2g.at[core, :, z, y], sems, 12 + o, zs[o]))
-    loads[1].wait()
-    for i in range(6):
-        csend[i] = cot[s6 + i]
-    cot_in = send(csend, cmate, sems, 8, mate)
-    fill_taps(taps, tapb, False)
-    clear_pads(xf)
-    clear_pads(df)
+    def pass_on(ch):
+        wait_all(third[ch])
+        return [send(w1g.at[core, ch], w1g.at[core, ch], sems, 101 + 2 * ch, mate),
+                send(w2g.at[core, ch], w2g.at[core, ch], sems, 102 + 2 * ch, mate)]
+    mate_in.wait()
+
+    def place_x(g):
+        lanes = slice(g * 128, g * 128 + 128)
+
+        def body(i, _):
+            p = p0 + i - 3
+            q = p - base
+            own = feat[jnp.clip(q, 0, CAP - 1), :, lanes].astype(F32)
+            other = xmate[jnp.clip(jnp.where(is_a, p - wa, p - off9), 0, 8), :, lanes].astype(F32)
+            edge = xhalo[g][jnp.clip(jnp.where(is_a, p + 3, p - pair), 0, 2)].astype(F32)
+            is_own = (q >= 0) & (q < mine)
+            is_edge = jnp.where(is_a, p < 0, p >= pair)
+            gone = (i >= n + 6) | (is_edge & jnp.where(is_a, me == 0, me == N_DEV - 1))
+            val = jnp.where(is_own, own, jnp.where(is_edge, edge, other))
+            xf[i, g, 8:8 + ROWS, :] = jnp.where(gone, 0.0, val)
+            return 0
+        lax.fori_loop(0, XC, body, 0)
+    halo_in[0].wait()
+    place_x(0)
+    conv_group(xf, tapb, conv, 0)
     wait_all(second)
     third = []
     for ch in range(3):
@@ -271,28 +297,15 @@
             copies.append(send(w1g.at[core, ch, z], w1g.at[core, ch, z], sems, 83 + ch * 6 + o, zs[o]))
             copies.append(send(w2g.at[core, ch, :, y], w2g.at[core, ch, :, y], sems, 83 + ch * 6 + 3 + o, ys[o]))
         third.append(copies)
-
-    def pass_on(ch):
-        wait_all(third[ch])
-        return [send(w1g.at[core, ch], w1g.at[core, ch], sems, 101 + 2 * ch, mate),
-                send(w2g.at[core, ch], w2g.at[core, ch], sems, 102 + 2 * ch, mate)]
-    wait_all(halo_in)
-
-    def place_x(i, _):
-        p = p0 + i - 3
-        q = p - base
-        own = feat[jnp.clip(q, 0, CAP - 1)].astype(F32)
-        other = xmate[jnp.clip(jnp.where(is_a, p - wa, p - off9), 0, 8)].astype(F32)
-        edge = xhalo[jnp.clip(jnp.where(is_a, p + 3, p - pair), 0, 2)].astype(F32)
-        is_own = (q >= 0) & (q < mine)
-        is_edge = jnp.where(is_a, p < 0, p >= pair)
-        gone = (i >= n + 6) | (is_edge & jnp.where(is_a, me == 0, me == N_DEV - 1))
-        val = jnp.where(is_own, own, jnp.where(is_edge, edge, other))
-        put_column(xf, i, jnp.where(gone, 0.0, val))
-        return 0
-    lax.fori_loop(0, XC, place_x, 0)
-    conv_group(xf, tapb, conv, 0)
-    cot_in.wait()
+    loads[1].wait()
+    for i in range(6):
+        csend[i] = cot[s6 + i]
+    cot_in = send(csend, cmate, sems, 8, mate)
+    halo_in[1].wait()
+    halo_in[2].wait()
+    place_x(1)
+    conv_group(xf, tapb, conv, 1)
+    place_x(2)
 
     def place_cot(j, _):
         p = p0 + j
@@ -302,10 +315,10 @@
         val = jnp.where((q >= 0) & (q < mine), own, other)
         cotb[j] = jnp.where(j >= n, 0.0, val).astype(BF16)
         return 0
+    conv_group(xf, tapb, conv, 2)
+    passed = [pass_on(0)]
+    cot_in.wait()
     lax.fori_loop(0, NC, place_cot, 0)
-    conv_group(xf, tapb, conv, 1)
-    passed = [pass_on(0)]
-    conv_group(xf, tapb, conv, 2)
     conv[NC - 1] = jnp.zeros((3, ROWS, 128), F32)
     vacc[...] = jnp.zeros_like(vacc)
     vecs = tuple(ref[...].astype(F32).reshape(1, C) for ref in (dw_bias, ln_gain, ln_bias, layer_scale))
@@ -381,30 +394,12 @@
         put_column(df, j + 3, dcv[j])
         return 0
     lax.fori_loop(0, NC, place_d, 0)
-    kernel_grads(xf, df, kacc, 0)
-    fill_taps(taps, tapf, True)
-    kernel_grads(xf, df, kacc, 1)
-    for copies in rs2:
-        wait_all(copies)
-    rs3 = []
-
-    def add_second(i, _):
-        ch, q = i // 4, lax.rem(i, 4)
-        t1[ch, q] = (c1[ch, z, q].astype(F32) + rz1[ch, 0, q].astype(F32) + rz1[ch, 1, q].astype(F32)
-                     + rz1[ch, 2, q].astype(F32)).astype(BF16)
-        t2[ch, q] = (c2[ch, q, y].astype(F32) + ry2[ch, 0, q].astype(F32) + ry2[ch, 1, q].astype(F32)
-                     + ry2[ch, 2, q].astype(F32)).astype(BF16)
-        return 0
-    lax.fori_loop(0, 12, add_second, 0)
-    for o in range(3):
-        rs3.append(send(t1.at[:, lax.rem(y + o + 1, 4)], ry1.at[o], sems, 33 + o, ys[o]))
-        rs3.append(send(t2.at[:, lax.rem(z + o + 1, 4)], rz2.at[o], sems, 36 + o, zs[o]))
-    kernel_grads(xf, df, kacc, 2)
-
+    for g in range(3):
+        kernel_grads(xf, df, kacc, g)
     def kout(i, _):
         krow[pl.ds(i, 1), :] = jnp.concatenate([jnp.sum(kacc[i, g], axis=0, keepdims=True) for g in range(3)], axis=1)
         return 0
-    lax.fori_loop(0, 49, kout, 0)
+    lax.fori_loop(0, 49, kout, 0, unroll=7)
     rows = [jnp.sum(vacc[i], axis=0, keepdims=True) for i in range(5)]
     krow[49:56, :] = jnp.zeros((7, C), F32)
     krow[56:64, :] = jnp.concatenate(rows + [jnp.zeros((3, C), F32)], axis=0)
@@ -425,10 +420,40 @@
             part_sum[stage + 1, h] = part_sum[stage, h] + slots[k] + slots[k + 1] + slots[k + 2]
 
     first_sum = send(cur.at[1 - core], mslot, sems, 46, mate)
+    for copies in rs2:
+        wait_all(copies)
+    rs3 = []
+
+    def add_second(i, _):
+        ch, q = i // 4, lax.rem(i, 4)
+        t1[ch, q] = (c1[ch, z, q].astype(F32) + rz1[ch, 0, q].astype(F32) + rz1[ch, 1, q].astype(F32)
+                     + rz1[ch, 2, q].astype(F32)).astype(BF16)
+        t2[ch, q] = (c2[ch, q, y].astype(F32) + ry2[ch, 0, q].astype(F32) + ry2[ch, 1, q].astype(F32)
+                     + ry2[ch, 2, q].astype(F32)).astype(BF16)
+        return 0
+    lax.fori_loop(0, 12, add_second, 0)
+    for o in range(3):
+        rs3.append(send(t1.at[:, lax.rem(y + o + 1, 4)], ry1.at[o], sems, 33 + o, ys[o]))
+        rs3.append(send(t2.at[:, lax.rem(z + o + 1, 4)], rz2.at[o], sems, 36 + o, zs[o]))
     first_sum.wait()
     for h in range(2):
         part_sum[0, h] = cur[core, h] + mslot[h]
     sums = sum_send(0, (ys, zs))
+    wait_all(halo_d)
+
+    def place_edges(i, _):
+        k = jnp.clip(i - n - 3, 0, 2)
+        left = jnp.where(is_a, dhalo[1, jnp.clip(i, 0, 2)].astype(F32), dhalo[0, jnp.clip(i, 0, 2)].astype(F32))
+        right = jnp.where(is_a, dhalo[0, k].astype(F32), dhalo[1, k].astype(F32))
+        left = jnp.where(me == 0, 0.0, left)
+        right = jnp.where((i >= n + 6) | (me == N_DEV - 1), 0.0, right)
+        own = dcv[jnp.clip(i - 3, 0, NC - 1)].astype(F32)
+        put_column(df, i, jnp.where(i < 3, left, jnp.where(i < n + 3, own, right)))
+        return 0
+    lax.fori_loop(0, XC, place_edges, 0)
+    back_group(df, tapf, cotb, dimg, 0)
+    sum_take(0, sums)
+    sums = sum_send(1, (zs, xs))
     wait_all(rs3)
     for ch in range(3):
         u1 = (t1[ch, y].astype(F32) + ry1[0, ch].astype(F32)) + (ry1[1, ch].astype(F32) + ry1[2, ch].astype(F32))
@@ -444,21 +469,6 @@
         q = lax.rem(x + o + 1, 4)
         rs4.append(send(p1.at[q], rx1.at[o], sems, 39 + o, xs[o]))
         rs4.append(send(p2.at[q], rx2.at[o], sems, 42 + o, xs[o]))
-    wait_all(halo_d)
-
-    def place_edges(i, _):
-        k = jnp.clip(i - n - 3, 0, 2)
-        left = jnp.where(is_a, dhalo[1, jnp.clip(i, 0, 2)].astype(F32), dhalo[0, jnp.clip(i, 0, 2)].astype(F32))
-        right = jnp.where(is_a, dhalo[0, k].astype(F32), dhalo[1, k].astype(F32))
-        left = jnp.where(me == 0, 0.0, left)
-        right = jnp.where((i >= n + 6) | (me == N_DEV - 1), 0.0, right)
-        own = dcv[jnp.clip(i - 3, 0, NC - 1)].astype(F32)
-        put_column(df, i, jnp.where(i < 3, left, jnp.where(i < n + 3, own, right)))
-        return 0
-    lax.fori_loop(0, XC, place_edges, 0)
-    back_group(df, tapf, cotb, dimg, 0)
-    sum_take(0, sums)
-    sums = sum_send(1, (zs, xs))
     back_group(df, tapf, cotb, dimg, 1)
     sum_take(1, sums)
     sums = sum_send(2, (xs, ys))
@@ -545,7 +555,7 @@
         out_specs=[VMEM] * 5,
         scratch_shapes=[
             v(CAP, ROWS, C), v(CAP, ROWS, C), v(16, 512), v(16, C), v(128, 128, dtype=F32),
-            v(9, ROWS, C), v(9, ROWS, C), v(3, ROWS, C), v(3, ROWS, C), v(6, ROWS, C), v(6, ROWS, C),
+            v(9, ROWS, C), v(9, ROWS, C), v(3, ROWS, C), v(3, ROWS, 128), v(3, ROWS, 128), v(3, ROWS, 128), v(6, ROWS, C), v(6, ROWS, C),
             v(4, 16, 512), v(4, 16, C), v(2, 3, 4, 4, 16, 512), v(2, 3, 4, 4, 16, C),
             v(XC, 3, RP, 128, dtype=F32), v(XC, 3, RP, 128, dtype=F32),
             v(49, 3, 8, 128, dtype=F32), v(49, 3, 8, 128, dtype=F32),

time: 84.3 us -> 80.8 us (0.958)
  Pallas kernels: 83.3 us -> 79.8 us
    pallas_call x1, Pallas kernels: 80 us -> 76.5 us  [fused(): pl.pallas_call(kernel, out_shape=(jax.ShapeDtypeStruct((NC, ROWS, C), BF1...]
where the time goes in v5:
time: 80.8 us; the launch traced here: 80.6 us
  Pallas kernels  79.8 us (99%)
  between operations  0.82 us (1%)
    pallas_call x1, Pallas kernels, fused(): pl.pallas_call(kernel, out_shape=(jax.ShapeDtypeStruct((NC, ROWS, C), BF1...  76.5 us
    pallas_call x1, Pallas kernels, finish(): pl.pallas_call(finish_kernel, out_shape=(f(CAP, ROWS, C, dtype=BF16), f(4...  3.3 us

profile of v5, /device:TPU:1, one launch (start us, length us, event | category | flops | bytes accessed | tf_op | source)
XLA Modules:
  0.0 80.6 jit_solution(1346616624503336494)
XLA Ops:
  0.6 76.5 %block_back.1 = (bf16[12,128,384]{2,1,0:T(8,128)(2,1)}, bf16[6,128,384]{2,1,0:T(8,128)(2,1)}, f32[64,384]{1,0:T(8,128)}, f32[16,512]{1,0:T(8,128)}, f32[16,384]{1,0:T(8,128)}) custom-call(s32[128]{0:T(128)} %widths.3, bf16[15,128,384]{2,1,0:T(8,128)(2,1)} %bitcast.6, bf16[15,128,384]{2,1,0:T(8,128)(2,1)} %bitcast.7, bf16[12,384]{1,0:T(8,128)(2,1)} %bitcast.8, ...), custom_call_target="tpu_custom_call" | custom-call | tf_op jit(solution)/shard_map/block_back/pallas_call | solution.py:545
  77.2 3.3 %place_results.1 = (bf16[15,128,384]{2,1,0:T(8,128)(2,1)}, f32[49,384]{1,0:T(8,128)}, f32[384]{0:T(512)}, f32[384]{0:T(512)}, f32[384]{0:T(512)}, /*index=5*/f32...) custom-call(s32[128]{0:T(128)} %widths.3, s32[1]{0:T(128)} %bitcast.place, ...), custom_call_target="tpu_custom_call" | custom-call | tf_op jit(solution)/shard_map/place_results/pallas_call | solution.py:532

commit v6 on v5

--- a/solution.py
+++ b/solution.py
@@ -107,7 +107,7 @@
                     if 0 <= i - b < NW:
                         accs[b] = accs[b] + ds[i - b] * xv
             return tuple(accs)
-        accs = lax.fori_loop(0, 16, rloop, tuple(jnp.zeros((8, 128), F32) for _ in range(7)), unroll=2)
+        accs = lax.fori_loop(0, 16, rloop, tuple(jnp.zeros((8, 128), F32) for _ in range(7)), unroll=8)
         for b in range(7):
             kacc[a * 7 + b, g] = accs[b]
         return 0
@@ -326,7 +326,7 @@
     def before(s, _):
         norm_step(s, conv, cotb, vecs, nrm, nrm_t, dm, dm_t, nraw_s, inv_s, vacc)
         return 0
-    lax.fori_loop(0, NC // 2, before, 0)
+    lax.fori_loop(0, NC // 2, before, 0, unroll=2)
 
     sums_w = [jnp.zeros((8, C), F32)]
     rs1, rs2 = {}, []
@@ -382,7 +382,7 @@
     def after(s, _):
         denorm_step(s, dn_s, nraw_s, inv_s, vecs[1], vacc, dcv)
         return 0
-    lax.fori_loop(0, NC // 2, after, 0)
+    lax.fori_loop(0, NC // 2, after, 0, unroll=2)
 
     last_at = jnp.maximum(n - 3, 0)
     inner_at, outer_at = jnp.where(is_a, last_at, 0), jnp.where(is_a, 0, last_at)
@@ -510,7 +510,7 @@
         val = jnp.where(is_own, own.astype(F32), other.astype(F32))
         d_out[s] = jnp.where(s >= mine, 0.0, val).astype(BF16)
         return 0
-    lax.fori_loop(0, CAP, place_out, 0)
+    lax.fori_loop(0, CAP, place_out, 0, unroll=3)
     g_kernel[...] = total[0:49]
 
     def row(i):

time: 80.8 us -> 79.2 us (0.980)
  Pallas kernels: 79.8 us -> 78.1 us
    pallas_call x1, Pallas kernels: 76.5 us -> 74.9 us  [fused(): pl.pallas_call(kernel, out_shape=(jax.ShapeDtypeStruct((NC, ROWS, C), BF1...]
where the time goes in v6:
time: 79.2 us; the launch traced here: 79 us
  Pallas kernels  78.1 us (99%)
  between operations  0.82 us (1%)
    pallas_call x1, Pallas kernels, fused(): pl.pallas_call(kernel, out_shape=(jax.ShapeDtypeStruct((NC, ROWS, C), BF1...  74.9 us
    pallas_call x1, Pallas kernels, finish(): pl.pallas_call(finish_kernel, out_shape=(f(CAP, ROWS, C, dtype=BF16), f(4...  3.22 us

profile of v6, /device:TPU:1, one launch (start us, length us, event | category | flops | bytes accessed | tf_op | source)
XLA Modules:
  0.0 79.0 jit_solution(3934046069270658483)
XLA Ops:
  0.6 74.9 %block_back.1 = (bf16[12,128,384]{2,1,0:T(8,128)(2,1)}, bf16[6,128,384]{2,1,0:T(8,128)(2,1)}, f32[64,384]{1,0:T(8,128)}, f32[16,512]{1,0:T(8,128)}, f32[16,384]{1,0:T(8,128)}) custom-call(s32[128]{0:T(128)} %widths.3, bf16[15,128,384]{2,1,0:T(8,128)(2,1)} %bitcast.6, bf16[15,128,384]{2,1,0:T(8,128)(2,1)} %bitcast.7, bf16[12,384]{1,0:T(8,128)(2,1)} %bitcast.8, ...), custom_call_target="tpu_custom_call" | custom-call | tf_op jit(solution)/shard_map/block_back/pallas_call | solution.py:545
  75.6 3.2 %place_results.1 = (bf16[15,128,384]{2,1,0:T(8,128)(2,1)}, f32[49,384]{1,0:T(8,128)}, f32[384]{0:T(512)}, f32[384]{0:T(512)}, f32[384]{0:T(512)}, /*index=5*/f32...) custom-call(s32[128]{0:T(128)} %widths.3, s32[1]{0:T(128)} %bitcast.place, ...), custom_call_target="tpu_custom_call" | custom-call | tf_op jit(solution)/shard_map/place_results/pallas_call | solution.py:532
